TPU v7x, 256 devices: a whole 4x4x8 slice. The times are simulated.
256 devices in a mesh: section: 32 (over y_hi, z, core), ctx: 8 (over y_lo, x).
Axes of the slice: x: 4, y: 4 (y_hi: 2, y_lo: 2; y = y_hi * 2 + y_lo), z: 8, core: 2. Of those that a mesh axis runs over, the one named last changes fastest.
Arguments:
- queries: bfloat16 [32, 1024, 8192], P('section', 'ctx'), may hold values from -6 to 6
- key_states: bfloat16 [32, 1024, 1024], P('section', 'ctx'), may hold values from -6 to 6
- value_states: bfloat16 [32, 1024, 1024], P('section', 'ctx'), may hold values from -1.5 to 1.5
- out_grad: bfloat16 [32, 1024, 8192], P('section', 'ctx'), may hold values from -6 to 6
- node_end: int32 [32, 1024], P('section'), may hold values from 1 to 1024, as said below
- block_list: int32 [32, 8, 8], P('section'), may hold values from 0 to 7, as said below
- block_count: int32 [32, 8], P('section'), may hold values from 1 to 8, as said below
Outputs:
- query_grads: bfloat16 [32, 1024, 8192], P('section', 'ctx')
- key_grads: bfloat16 [32, 1024, 1024], P('section', 'ctx')
- value_grads: bfloat16 [32, 1024, 1024], P('section', 'ctx')
Inputs may be any that keep to these rules, and one draw needn't show every extreme that they name: Each section packs search trees one after another, each in preorder; node_end[s, j] is one past the last node of node j's subtree, so j is an ancestor of i (or i itself) exactly when j <= i < node_end[s, j]. Row b of block_list[s] lists, in increasing order, every key block that holds an ancestor (or the node itself) of some node of query block b, and no other; b itself is always listed; entries after the first block_count[s, b] are 0. block_count[s, b] is the number of listed key blocks of query block b, at most b + 1.
All inputs are finite; a program needn't handle non-finite values.
Results may differ from a plain program's by a relative error of at most 0.0053.
Values may be sent and summed in bfloat16 or wider, within the bound.
No kernel may reach another device: no remote copies, remote signals or barrier semaphores. Data moves between devices by JAX's collectives and lax.ppermute only.
A program may use at most 128 MiB of HBM per device.

v0:
```python
import math

import jax
import jax.numpy as jnp
from jax import lax
from jax.sharding import PartitionSpec as P

HEADS = 64
KV_HEADS = 8
HEAD_DIM = 128
BLK = 128


def from_behind(block, axis, distance):
    devices = range(lax.axis_size(axis))
    route = [((i - distance) % len(devices), i) for i in devices]
    return lax.ppermute(block, axis, route)


def allowed_mask(end_row, list_rows, count_row):
    length = end_row.shape[0]
    block_total = list_rows.shape[0]
    position = jnp.arange(length, dtype=jnp.int32)
    ancestry = (position[None, :] <= position[:, None]) & (position[:, None] < end_row[None, :])
    entries = jnp.arange(block_total, dtype=jnp.int32)
    listed = jnp.any(
        (list_rows[:, :, None] == entries[None, None, :])
        & (entries[None, :, None] < count_row[:, None, None]),
        axis=1,
    )
    spread = jnp.repeat(jnp.repeat(listed, BLK, axis=0), BLK, axis=1)
    return ancestry & spread


def head_block(query_rows, grad_rows, key_rows, value_rows, allowed):
    row_total = query_rows.shape[0]
    scale = 1.0 / math.sqrt(HEAD_DIM)
    query_heads = query_rows.reshape(row_total, -1, HEAD_DIM)
    grad_heads = grad_rows.reshape(row_total, -1, HEAD_DIM)
    scores = (
        jnp.einsum("qhd,kd->hqk", query_heads, key_rows, preferred_element_type=jnp.float32) * scale
    )
    scores = jnp.where(allowed[None], scores, -jnp.inf)
    row_max = jnp.max(scores, axis=2, keepdims=True)
    exponent = jnp.exp(scores - row_max)
    attention = exponent / jnp.sum(exponent, axis=2, keepdims=True)
    attention_half = attention.astype(jnp.bfloat16)
    weight_grad = jnp.einsum(
        "qhd,kd->hqk", grad_heads, value_rows, preferred_element_type=jnp.float32
    )
    row_delta = jnp.sum(attention * weight_grad, axis=2, keepdims=True)
    score_grad = (attention * (weight_grad - row_delta) * scale).astype(jnp.bfloat16)
    query_grad = jnp.einsum(
        "hqk,kd->qhd", score_grad, key_rows, preferred_element_type=jnp.float32
    ).reshape(row_total, -1)
    key_grad = jnp.einsum(
        "hqk,qhd->kd", score_grad, query_heads, preferred_element_type=jnp.float32
    )
    value_grad = jnp.einsum(
        "hqk,qhd->kd", attention_half, grad_heads, preferred_element_type=jnp.float32
    )
    return (query_grad, key_grad, value_grad)


def per_device(queries, key_states, value_states, out_grad, node_end, block_list, block_count):
    node_count = queries.shape[1]
    allowed = allowed_mask(node_end[0], block_list[0], block_count[0])
    ratio = HEADS // KV_HEADS
    full_keys, full_values = (
        lax.all_gather(key_states, "ctx", axis=1, tiled=True),
        lax.all_gather(value_states, "ctx", axis=1, tiled=True),
    )
    length = full_keys.shape[1]
    row_allowed = lax.dynamic_slice_in_dim(
        allowed, lax.axis_index("ctx") * node_count, node_count, 0
    )
    width = ratio * HEAD_DIM

    def per_group(group_index, carry):
        query_acc, pair_acc = carry
        query_grad, key_grad, value_grad = head_block(
            lax.dynamic_slice_in_dim(queries[0], group_index * width, width, 1),
            lax.dynamic_slice_in_dim(out_grad[0], group_index * width, width, 1),
            lax.dynamic_slice_in_dim(full_keys[0], group_index * HEAD_DIM, HEAD_DIM, 1),
            lax.dynamic_slice_in_dim(full_values[0], group_index * HEAD_DIM, HEAD_DIM, 1),
            row_allowed,
        )
        query_acc = lax.dynamic_update_slice_in_dim(
            query_acc, query_grad.astype(jnp.bfloat16), group_index * width, 1
        )
        pair_acc = lax.dynamic_update_slice_in_dim(
            pair_acc, jnp.stack([key_grad, value_grad]), group_index * HEAD_DIM, 2
        )
        return (query_acc, pair_acc)

    start_query = jnp.zeros((node_count, queries.shape[2]), jnp.bfloat16)
    start_pair = jnp.zeros((2, length, key_states.shape[2]), jnp.float32)
    query_acc, pair_acc = lax.fori_loop(0, KV_HEADS, per_group, (start_query, start_pair))
    summed = lax.psum_scatter(pair_acc, "ctx", scatter_dimension=1, tiled=True)
    query_nodes = query_acc[None]
    pair_nodes = summed.astype(jnp.bfloat16)
    query_sent = from_behind(query_nodes, "section", -1)
    pair_sent = from_behind(pair_nodes, "section", -1)
    return (query_sent, pair_sent[0:1], pair_sent[1:2])


def solution(mesh):
    placed = (
        P("section", "ctx", None),
        P("section", "ctx", None),
        P("section", "ctx", None),
        P("section", "ctx", None),
        P("section", None),
        P("section", None, None),
        P("section", None),
    )
    return jax.shard_map(
        per_device,
        mesh=mesh,
        in_specs=placed,
        out_specs=(P("section", "ctx", None), P("section", "ctx", None), P("section", "ctx", None)),
        check_vma=False,
    )
```

profile of v0, /device:TPU:2, one launch (start us, length us, event | category | flops | bytes accessed | tf_op | source)
XLA Modules:
  0.0 457.6 jit_solution(3999073993154204466)
XLA Ops:
  11.5 43.0 %all-gather.3.cloned.1.call-done = bf16[1,1024,1024]{2,1,0:T(8,128)(2,1)} async-done(((bf16[1,128,1024]{2,1,0:T(8,128)(2,1)}), bf16[1,1024,1024]{2,1,0:T(8,128)(2,1)}) %all-gather.3.cloned.1.call-update) | async-done | bytes 2097168 | tf_op jit(solution)/shard_map/all_gather | solution.py:70
  54.5 45.2 %all-gather.5.cloned.1.call-done = bf16[1,1024,1024]{2,1,0:T(8,128)(2,1)} async-done(((bf16[1,128,1024]{2,1,0:T(8,128)(2,1)}), bf16[1,1024,1024]{2,1,0:T(8,128)(2,1)}) %all-gather.5.cloned.1.call-update) | async-done | bytes 2097168 | tf_op jit(solution)/shard_map/all_gather | solution.py:71
  101.2 4.3 broadcast_in_dim.57
  105.5 228.4 %while.15 = (s32[]{:T(128)}, bf16[128,8192]{1,0:T(8,128)(2,1)}, f32[2,1024,1024]{2,1,0:T(8,128)}, bf16[1,1024,1024]{2,1,0:T(8,128)(2,1)}, pred[128,1024]{0,1:T(8...) while((s32[]{:T(128)}, bf16[128,8192]{1,0:T(8,128)(2,1)}, ...), condition=%wide.region_5.6_spmd, body=%wide.region_1.5_spmd.sunk | while | flops 1363547136 | bytes 46289144 | solution.py:98
  114.8 7.1 %fusion.91 = f32[1,1024,128]{2,1,0:T(8,128)S(1)} fusion(bf16[128,8,128]{0,2,1:T(8,128)(2,1)S(1)} %bitcast.121, f32[1024,128,8]{1,0,2:T(8,128)} %fusion.87, f32[8,128,1024]{1,2,0:T(8,128)} %get-tuple-element.238, f32[8,128]{1,0:T(8,128)S(1)} %get-tuple-element.239), kind=kOutput, calls=%fused_computation.19.clone.1 | convolution fusion | flops 275777536 | bytes 9179136 | tf_op jit(solution)/shard_map/while/body/eval_jaxpr/hqk,qhd->kd/dot_general | solution.py:56
  121.9 7.3 %fusion.89 = bf16[128,8,128]{2,0,1:T(8,128)(2,1)S(1)} fusion(f32[1024,128,8]{1,0,2:T(8,128)} %fusion.87, bf16[1,1024,1024]{2,1,0:T(8,128)(2,1)} %get-tuple-element.269, s32[]{:T(128)S(6)} %select_n.45, f32[8,128,1024]{1,2,0:T(8,128)} %get-tuple-element.238, f32[8,128]{1,0:T(8,128)S(1)} %get-tuple-element.239), kind=kOutput, calls=%fused_computation.21.clone.1 | convolution fusion | flops 275908608 | bytes 17309700 | tf_op jit(solution)/shard_map/while/body/eval_jaxpr/hqk,kd->qhd/dot_general | solution.py:53
  143.4 7.1 %fusion.91 = f32[1,1024,128]{2,1,0:T(8,128)S(1)} fusion(bf16[128,8,128]{0,2,1:T(8,128)(2,1)S(1)} %bitcast.121, f32[1024,128,8]{1,0,2:T(8,128)} %fusion.87, f32[8,128,1024]{1,2,0:T(8,128)} %get-tuple-element.238, f32[8,128]{1,0:T(8,128)S(1)} %get-tuple-element.239), kind=kOutput, calls=%fused_computation.19.clone.1 | convolution fusion | flops 275777536 | bytes 9179136 | tf_op jit(solution)/shard_map/while/body/eval_jaxpr/hqk,qhd->kd/dot_general | solution.py:56
  150.4 7.3 %fusion.89 = bf16[128,8,128]{2,0,1:T(8,128)(2,1)S(1)} fusion(f32[1024,128,8]{1,0,2:T(8,128)} %fusion.87, bf16[1,1024,1024]{2,1,0:T(8,128)(2,1)} %get-tuple-element.269, s32[]{:T(128)S(6)} %select_n.45, f32[8,128,1024]{1,2,0:T(8,128)} %get-tuple-element.238, f32[8,128]{1,0:T(8,128)S(1)} %get-tuple-element.239), kind=kOutput, calls=%fused_computation.21.clone.1 | convolution fusion | flops 275908608 | bytes 17309700 | tf_op jit(solution)/shard_map/while/body/eval_jaxpr/hqk,kd->qhd/dot_general | solution.py:53
  171.9 7.1 %fusion.91 = f32[1,1024,128]{2,1,0:T(8,128)S(1)} fusion(bf16[128,8,128]{0,2,1:T(8,128)(2,1)S(1)} %bitcast.121, f32[1024,128,8]{1,0,2:T(8,128)} %fusion.87, f32[8,128,1024]{1,2,0:T(8,128)} %get-tuple-element.238, f32[8,128]{1,0:T(8,128)S(1)} %get-tuple-element.239), kind=kOutput, calls=%fused_computation.19.clone.1 | convolution fusion | flops 275777536 | bytes 9179136 | tf_op jit(solution)/shard_map/while/body/eval_jaxpr/hqk,qhd->kd/dot_general | solution.py:56
  179.0 7.3 %fusion.89 = bf16[128,8,128]{2,0,1:T(8,128)(2,1)S(1)} fusion(f32[1024,128,8]{1,0,2:T(8,128)} %fusion.87, bf16[1,1024,1024]{2,1,0:T(8,128)(2,1)} %get-tuple-element.269, s32[]{:T(128)S(6)} %select_n.45, f32[8,128,1024]{1,2,0:T(8,128)} %get-tuple-element.238, f32[8,128]{1,0:T(8,128)S(1)} %get-tuple-element.239), kind=kOutput, calls=%fused_computation.21.clone.1 | convolution fusion | flops 275908608 | bytes 17309700 | tf_op jit(solution)/shard_map/while/body/eval_jaxpr/hqk,kd->qhd/dot_general | solution.py:53
  200.5 7.1 %fusion.91 = f32[1,1024,128]{2,1,0:T(8,128)S(1)} fusion(bf16[128,8,128]{0,2,1:T(8,128)(2,1)S(1)} %bitcast.121, f32[1024,128,8]{1,0,2:T(8,128)} %fusion.87, f32[8,128,1024]{1,2,0:T(8,128)} %get-tuple-element.238, f32[8,128]{1,0:T(8,128)S(1)} %get-tuple-element.239), kind=kOutput, calls=%fused_computation.19.clone.1 | convolution fusion | flops 275777536 | bytes 9179136 | tf_op jit(solution)/shard_map/while/body/eval_jaxpr/hqk,qhd->kd/dot_general | solution.py:56
  207.5 7.3 %fusion.89 = bf16[128,8,128]{2,0,1:T(8,128)(2,1)S(1)} fusion(f32[1024,128,8]{1,0,2:T(8,128)} %fusion.87, bf16[1,1024,1024]{2,1,0:T(8,128)(2,1)} %get-tuple-element.269, s32[]{:T(128)S(6)} %select_n.45, f32[8,128,1024]{1,2,0:T(8,128)} %get-tuple-element.238, f32[8,128]{1,0:T(8,128)S(1)} %get-tuple-element.239), kind=kOutput, calls=%fused_computation.21.clone.1 | convolution fusion | flops 275908608 | bytes 17309700 | tf_op jit(solution)/shard_map/while/body/eval_jaxpr/hqk,kd->qhd/dot_general | solution.py:53
  229.0 7.1 %fusion.91 = f32[1,1024,128]{2,1,0:T(8,128)S(1)} fusion(bf16[128,8,128]{0,2,1:T(8,128)(2,1)S(1)} %bitcast.121, f32[1024,128,8]{1,0,2:T(8,128)} %fusion.87, f32[8,128,1024]{1,2,0:T(8,128)} %get-tuple-element.238, f32[8,128]{1,0:T(8,128)S(1)} %get-tuple-element.239), kind=kOutput, calls=%fused_computation.19.clone.1 | convolution fusion | flops 275777536 | bytes 9179136 | tf_op jit(solution)/shard_map/while/body/eval_jaxpr/hqk,qhd->kd/dot_general | solution.py:56
  236.1 7.3 %fusion.89 = bf16[128,8,128]{2,0,1:T(8,128)(2,1)S(1)} fusion(f32[1024,128,8]{1,0,2:T(8,128)} %fusion.87, bf16[1,1024,1024]{2,1,0:T(8,128)(2,1)} %get-tuple-element.269, s32[]{:T(128)S(6)} %select_n.45, f32[8,128,1024]{1,2,0:T(8,128)} %get-tuple-element.238, f32[8,128]{1,0:T(8,128)S(1)} %get-tuple-element.239), kind=kOutput, calls=%fused_computation.21.clone.1 | convolution fusion | flops 275908608 | bytes 17309700 | tf_op jit(solution)/shard_map/while/body/eval_jaxpr/hqk,kd->qhd/dot_general | solution.py:53
  253.3 4.3 fusion.88
  257.5 7.1 %fusion.91 = f32[1,1024,128]{2,1,0:T(8,128)S(1)} fusion(bf16[128,8,128]{0,2,1:T(8,128)(2,1)S(1)} %bitcast.121, f32[1024,128,8]{1,0,2:T(8,128)} %fusion.87, f32[8,128,1024]{1,2,0:T(8,128)} %get-tuple-element.238, f32[8,128]{1,0:T(8,128)S(1)} %get-tuple-element.239), kind=kOutput, calls=%fused_computation.19.clone.1 | convolution fusion | flops 275777536 | bytes 9179136 | tf_op jit(solution)/shard_map/while/body/eval_jaxpr/hqk,qhd->kd/dot_general | solution.py:56
  264.6 7.3 %fusion.89 = bf16[128,8,128]{2,0,1:T(8,128)(2,1)S(1)} fusion(f32[1024,128,8]{1,0,2:T(8,128)} %fusion.87, bf16[1,1024,1024]{2,1,0:T(8,128)(2,1)} %get-tuple-element.269, s32[]{:T(128)S(6)} %select_n.45, f32[8,128,1024]{1,2,0:T(8,128)} %get-tuple-element.238, f32[8,128]{1,0:T(8,128)S(1)} %get-tuple-element.239), kind=kOutput, calls=%fused_computation.21.clone.1 | convolution fusion | flops 275908608 | bytes 17309700 | tf_op jit(solution)/shard_map/while/body/eval_jaxpr/hqk,kd->qhd/dot_general | solution.py:53
  286.1 7.1 %fusion.91 = f32[1,1024,128]{2,1,0:T(8,128)S(1)} fusion(bf16[128,8,128]{0,2,1:T(8,128)(2,1)S(1)} %bitcast.121, f32[1024,128,8]{1,0,2:T(8,128)} %fusion.87, f32[8,128,1024]{1,2,0:T(8,128)} %get-tuple-element.238, f32[8,128]{1,0:T(8,128)S(1)} %get-tuple-element.239), kind=kOutput, calls=%fused_computation.19.clone.1 | convolution fusion | flops 275777536 | bytes 9179136 | tf_op jit(solution)/shard_map/while/body/eval_jaxpr/hqk,qhd->kd/dot_general | solution.py:56
  293.2 7.3 %fusion.89 = bf16[128,8,128]{2,0,1:T(8,128)(2,1)S(1)} fusion(f32[1024,128,8]{1,0,2:T(8,128)} %fusion.87, bf16[1,1024,1024]{2,1,0:T(8,128)(2,1)} %get-tuple-element.269, s32[]{:T(128)S(6)} %select_n.45, f32[8,128,1024]{1,2,0:T(8,128)} %get-tuple-element.238, f32[8,128]{1,0:T(8,128)S(1)} %get-tuple-element.239), kind=kOutput, calls=%fused_computation.21.clone.1 | convolution fusion | flops 275908608 | bytes 17309700 | tf_op jit(solution)/shard_map/while/body/eval_jaxpr/hqk,kd->qhd/dot_general | solution.py:53
  314.7 7.1 %fusion.91 = f32[1,1024,128]{2,1,0:T(8,128)S(1)} fusion(bf16[128,8,128]{0,2,1:T(8,128)(2,1)S(1)} %bitcast.121, f32[1024,128,8]{1,0,2:T(8,128)} %fusion.87, f32[8,128,1024]{1,2,0:T(8,128)} %get-tuple-element.238, f32[8,128]{1,0:T(8,128)S(1)} %get-tuple-element.239), kind=kOutput, calls=%fused_computation.19.clone.1 | convolution fusion | flops 275777536 | bytes 9179136 | tf_op jit(solution)/shard_map/while/body/eval_jaxpr/hqk,qhd->kd/dot_general | solution.py:56
  321.7 7.3 %fusion.89 = bf16[128,8,128]{2,0,1:T(8,128)(2,1)S(1)} fusion(f32[1024,128,8]{1,0,2:T(8,128)} %fusion.87, bf16[1,1024,1024]{2,1,0:T(8,128)(2,1)} %get-tuple-element.269, s32[]{:T(128)S(6)} %select_n.45, f32[8,128,1024]{1,2,0:T(8,128)} %get-tuple-element.238, f32[8,128]{1,0:T(8,128)S(1)} %get-tuple-element.239), kind=kOutput, calls=%fused_computation.21.clone.1 | convolution fusion | flops 275908608 | bytes 17309700 | tf_op jit(solution)/shard_map/while/body/eval_jaxpr/hqk,kd->qhd/dot_general | solution.py:53
  337.5 91.2 %reduce-scatter.2.cloned.1.call-done = f32[2,128,1024]{2,1,0:T(8,128)} async-done(((f32[2,1024,1024]{2,1,0:T(8,128)}), f32[2,128,1024]{2,1,0:T(8,128)}) %reduce-scatter.2.cloned.1.call-update) | async-done | bytes 1048592 | tf_op jit(solution)/shard_map/reduce_scatter | solution.py:99
  430.0 10.5 %collective-permute-start.1 = (bf16[2,128,1024]{2,1,0:T(8,128)(2,1)S(1)}, bf16[2,128,1024]{2,1,0:T(8,128)(2,1)S(1)}, u32[]{:S(2)}, u32[]{:S(2)}) collective-permute-start(bf16[2,128,1024]{2,1,0:T(8,128)(2,1)S(1)} %convert_element_type.30), channel_id=1, source_target_pairs={{8,0},{16,8},{24,16},{32,24},{40,32},{48,40},{56,48},{64,56},{72,6... | collective-permute-start | bytes 1572872 | tf_op jit(solution)/shard_map/ppermute | solution.py:17
  440.5 6.7 %collective-permute-done.1 = bf16[2,128,1024]{2,1,0:T(8,128)(2,1)S(1)} collective-permute-done((bf16[2,128,1024]{2,1,0:T(8,128)(2,1)S(1)}, bf16[2,128,1024]{2,1,0:T(8,128)(2,1)S(1)}, u32[]{:S(2)}, u32[]{:S(2)}) %collective-permute-start.1) | collective-permute-done | bytes 524320 | tf_op jit(solution)/shard_map/ppermute | solution.py:17
  (90 shorter events, 123.7 us)
Async XLA Ops:
  7.2 47.4 %all-gather.3.cloned.1.call-start = ((), (), s32[]{:S(2)}) async-start(), calls=%async_computation.1 | async-start | bytes 2359296 | tf_op jit(solution)/shard_map/all_gather | solution.py:70
  7.9 91.8 %all-gather.5.cloned.1.call-start = ((), (), s32[]{:S(2)}) async-start(), calls=%async_computation.2 | async-start | bytes 2359296 | tf_op jit(solution)/shard_map/all_gather | solution.py:71
  8.6 420.1 %reduce-scatter.2.cloned.1.call-start = ((), (), s32[]{:S(2)}) async-start(), calls=%async_computation.3 | async-start | bytes 9437184 | tf_op jit(solution)/shard_map/reduce_scatter | solution.py:99
  333.9 1.6 copy-start
  335.5 105.0 %collective-permute-start = (bf16[1,128,8192]{2,1,0:T(8,128)(2,1)S(1)}, bf16[1,128,8192]{2,1,0:T(8,128)(2,1)}, u32[]{:S(2)}, u32[]{:S(2)}) collective-permute-start(bf16[1,128,8192]{2,1,0:T(8,128)(2,1)S(1)} %bitcast.123), channel_id=1, source_target_pairs={{8,0},{16,8},{24,16},{32,24},{40,32},{48,40},{56,48},{64,56},{72,6... | collective-permute-start | bytes 6291464 | tf_op jit(solution)/shard_map/ppermute | solution.py:17
  430.0 17.2 %collective-permute-start.1 = (bf16[2,128,1024]{2,1,0:T(8,128)(2,1)S(1)}, bf16[2,128,1024]{2,1,0:T(8,128)(2,1)S(1)}, u32[]{:S(2)}, u32[]{:S(2)}) collective-permute-start(bf16[2,128,1024]{2,1,0:T(8,128)(2,1)S(1)} %convert_element_type.30), channel_id=1, source_target_pairs={{8,0},{16,8},{24,16},{32,24},{40,32},{48,40},{56,48},{64,56},{72,6... | collective-permute-start | bytes 1572872 | tf_op jit(solution)/shard_map/ppermute | solution.py:17
Sparse Core Ops, SparseCore 0:
  9.8 44.6 all-gather.2
  56.3 43.3 all-gather.4
  334.0 94.6 reduce-scatter.1
where the time goes:
time: 466 us; the launch traced here: 458 us
  matrix products  201 us (43%)
  waiting for transfers between devices  187 us (40%)
  local copies, waits for them, and re-layouts  29.9 us (6%)
  between operations  13.8 us (3%)
  starting transfers between devices  12.7 us (3%)
  other arithmetic  12.6 us (3%)
    reduce_scatter x1, waiting for transfers between devices, per_device(): summed = lax.psum_scatter(pair_acc, 'ctx', scatter_dimension=1, tiled=True)  91.2 us
    dot_general x8, matrix products, head_block(): jnp.einsum('hqk,kd->qhd', score_grad, key_rows, preferred_element_type=jn...  58.1 us
    dot_general x8, matrix products, head_block(): jnp.einsum('hqk,qhd->kd', score_grad, query_heads, preferred_element_type...  56.6 us
    all_gather x1, waiting for transfers between devices, per_device(): lax.all_gather(value_states, 'ctx', axis=1, tiled=True)  45.2 us
    all_gather x1, waiting for transfers between devices, per_device(): lax.all_gather(key_states, 'ctx', axis=1, tiled=True)  43 us
    sub x8, matrix products, head_block(): exponent = jnp.exp(scores - row_max)  34 us
    dot_general x8, matrix products, head_block(): jnp.einsum('qhd,kd->hqk', grad_heads, value_rows, preferred_element_type=...  29 us
    dot_general x8, matrix products, head_block(): jnp.einsum('hqk,qhd->kd', attention_half, grad_heads, preferred_element_t...  23.1 us
  transfers between devices with their start and end apart: 5, of which 4 were waited for; matrix products, arithmetic and copies ran while one was open for 1% of the time, Pallas kernels for 0%

commit v1 on v0

v1 whole, which is shorter than its diff:
```python
import functools
import math

import jax
import jax.numpy as jnp
from jax import lax
from jax.experimental import pallas as pl
from jax.experimental.pallas import tpu as pltpu
from jax.sharding import PartitionSpec as P

HEADS = 64
KV_HEADS = 8
HEAD_DIM = 128
BLK = 128
NBLK = 8
RATIO = HEADS // KV_HEADS
LANES = RATIO * BLK
HALF = 2 * BLK
RING = 4
CHUNKS = 2
GROUPS = KV_HEADS // CHUNKS
SCALE = 1.0 / math.sqrt(HEAD_DIM)
LOG2E = math.log2(math.e)
LOWEST = -3.0e38


def ctx_route(move):
    route = []
    for place in range(NBLK):
        target = move(place // RING, place % RING)
        if target is not None:
            route.append((place, target[0] * RING + target[1] % RING))
    return route


def right(y, x):
    return (y, x + 1)


def left(y, x):
    return (y, x - 1)


def across(y, x):
    return (y, x + 2)


def up(y, x):
    return (1, x) if y == 0 else None


def down(y, x):
    return (0, x) if y == 1 else None


def stay(y, x):
    return (y, x)


def send(block, move):
    return lax.ppermute(block, "ctx", ctx_route(move))


def send_behind(block, move):
    sections = lax.axis_size("section")
    route = []
    for section in range(sections):
        for source, target in ctx_route(move):
            route.append((section * NBLK + source, ((section - 1) % sections) * NBLK + target))
    return lax.ppermute(block, ("section", "ctx"), route)


def nt_dot(a, b):
    return lax.dot_general(a, b, (((1,), (1,)), ((), ())), preferred_element_type=jnp.float32)


def grads_kernel(info, ends_ref, q_ref, g_ref, own_ref, left_ref, right_ref, y_ref, x2_ref, ylr_ref,
                 dq_ref, near_ref, far_ref, side_ref,
                 keys, values, bias, weights, wgrads, tops, dq_acc, pair_acc):
    count = info[0]
    row_place = info[9]
    y = row_place // RING
    x = lax.rem(row_place, RING)
    other = 1 - y
    pairs = lax.div(count + 1, 2)

    def place_of(row, column):
        return row * RING + lax.rem(column + RING, RING)

    @pl.when(pl.program_id(0) == 0)
    def _():
        row = row_place * BLK + lax.broadcasted_iota(jnp.int32, (BLK, BLK), 1)
        inner = lax.broadcasted_iota(jnp.int32, (BLK, BLK), 0)
        for entry in range(NBLK):
            block = info[1 + entry]
            column = block * BLK + inner
            ends = ends_ref[pl.ds(pl.multiple_of(block * BLK, BLK), BLK), :]
            good = (column <= row) & (row < ends) & (entry < count)
            bias[pl.ds(entry * BLK, BLK), :] = jnp.where(good, 0.0, -jnp.inf)

    slots = (
        (own_ref, (), place_of(y, x)),
        (left_ref, (), place_of(y, x - 1)),
        (right_ref, (), place_of(y, x + 1)),
        (y_ref, (), place_of(other, x)),
        (x2_ref, (0,), place_of(y, x + 2)),
        (x2_ref, (1,), place_of(other, x + 2)),
        (ylr_ref, (0,), place_of(other, x - 1)),
        (ylr_ref, (1,), place_of(other, x + 1)),
    )
    for ref, lead, place in slots:
        rows = pl.ds(pl.multiple_of(place * BLK, BLK), BLK)
        keys[rows, :] = ref[(*lead, 0)]
        values[rows, :] = ref[(*lead, 1)]

    pair_acc[...] = jnp.zeros_like(pair_acc)
    dq_acc[...] = jnp.zeros_like(dq_acc)

    def block_rows(entry):
        return pl.ds(pl.multiple_of(info[1 + entry] * BLK, BLK), BLK)

    def both(ref, pair):
        return jnp.concatenate([ref[block_rows(2 * pair), :], ref[block_rows(2 * pair + 1), :]], axis=0)

    def two_heads(ref, part):
        first = part * HALF
        return jnp.concatenate([ref[0, :, first:first + BLK], ref[0, :, first + BLK:first + HALF]], axis=0)

    def first_pass(pair, carry):
        top, total, delta = carry
        key_pair = both(keys, pair)
        value_pair = both(values, pair)
        rows = pl.ds(pl.multiple_of(pair * HALF, HALF), HALF)
        mask = bias[rows, :]
        mask2 = jnp.concatenate([mask, mask], axis=1)
        new_top, new_total, new_delta = [], [], []
        for part in range(RATIO // 2):
            lanes = slice(part * HALF, (part + 1) * HALF)
            scores = nt_dot(key_pair, two_heads(q_ref, part)) + mask2
            wgrad = nt_dot(value_pair, two_heads(g_ref, part))
            old = top[:, lanes]
            now = jnp.maximum(old, jnp.max(scores, axis=0, keepdims=True))
            weight = jnp.exp2((scores - now) * (SCALE * LOG2E))
            shrink = jnp.exp2((old - now) * (SCALE * LOG2E))
            weights[rows, lanes] = weight
            wgrads[rows, lanes] = wgrad
            new_top.append(now)
            new_total.append(total[:, lanes] * shrink + jnp.sum(weight, axis=0, keepdims=True))
            new_delta.append(delta[:, lanes] * shrink + jnp.sum(weight * wgrad, axis=0, keepdims=True))
        top = jnp.concatenate(new_top, axis=1)
        tops[pl.ds(pair, 1), :] = top
        return (top, jnp.concatenate(new_total, axis=1), jnp.concatenate(new_delta, axis=1))

    zero = jnp.zeros((1, LANES), jnp.float32)
    top, total, delta = lax.fori_loop(0, pairs, first_pass, (jnp.full((1, LANES), LOWEST, jnp.float32), zero, zero))
    inverse = 1.0 / total
    delta = delta * inverse

    def second_pass(pair, carry):
        key_pair_t = both(keys, pair).T
        rows = pl.ds(pl.multiple_of(pair * HALF, HALF), HALF)
        factor = jnp.exp2((tops[pl.ds(pair, 1), :] - top) * (SCALE * LOG2E)) * inverse
        key_sum = jnp.zeros((HALF, HEAD_DIM), jnp.float32)
        value_sum = jnp.zeros((HALF, HEAD_DIM), jnp.float32)
        for part in range(RATIO // 2):
            lanes = slice(part * HALF, (part + 1) * HALF)
            attention = weights[rows, lanes] * factor[:, lanes]
            score_grad = (attention * ((wgrads[rows, lanes] - delta[:, lanes]) * SCALE)).astype(jnp.bfloat16)
            value_sum += jnp.dot(attention.astype(jnp.bfloat16), two_heads(g_ref, part), preferred_element_type=jnp.float32)
            key_sum += jnp.dot(score_grad, two_heads(q_ref, part), preferred_element_type=jnp.float32)
            dq_acc[:, lanes] += jnp.dot(key_pair_t, score_grad, preferred_element_type=jnp.float32)

        pair_acc[0, block_rows(2 * pair), :] = key_sum[:BLK]
        pair_acc[1, block_rows(2 * pair), :] = value_sum[:BLK]

        @pl.when(2 * pair + 1 < count)
        def _():
            pair_acc[0, block_rows(2 * pair + 1), :] = key_sum[BLK:]
            pair_acc[1, block_rows(2 * pair + 1), :] = value_sum[BLK:]

        return carry

    lax.fori_loop(0, pairs, second_pass, 0)
    for head in range(RATIO):
        lanes = slice(head * BLK, (head + 1) * BLK)
        dq_ref[:, lanes] = dq_acc[:, lanes].T.astype(jnp.bfloat16)
    outs = (
        (near_ref, (0,), slots[0][2]),
        (near_ref, (1,), slots[1][2]),
        (near_ref, (2,), slots[2][2]),
        (near_ref, (3,), slots[3][2]),
        (far_ref, (0,), slots[4][2]),
        (far_ref, (1,), slots[5][2]),
        (side_ref, (0,), slots[6][2]),
        (side_ref, (1,), slots[7][2]),
    )
    for ref, lead, place in outs:
        rows = pl.ds(pl.multiple_of(place * BLK, BLK), BLK)
        for which in range(2):
            ref[(*lead, which)] = pair_acc[which, rows, :].astype(ref.dtype)


def chunk_grads(chunk, info, ends, queries, out_grad, own, from_left, from_right, from_y, from_x2, from_ylr):
    width = LANES
    wide = pl.BlockSpec((1, BLK, width), lambda g, *_: (0, 0, chunk * GROUPS + g))
    one = pl.BlockSpec((2, BLK, HEAD_DIM), lambda g, *_: (0, 0, g))
    two = pl.BlockSpec((2, 2, BLK, HEAD_DIM), lambda g, *_: (0, 0, 0, g))
    four = pl.BlockSpec((4, 2, BLK, HEAD_DIM), lambda g, *_: (0, 0, 0, g))
    columns = GROUPS * HEAD_DIM
    return pl.pallas_call(
        grads_kernel,
        grid_spec=pltpu.PrefetchScalarGridSpec(
            num_scalar_prefetch=1,
            grid=(GROUPS,),
            in_specs=[pl.BlockSpec((NBLK * BLK, 1), lambda g, *_: (0, 0)), wide, wide, one, one, one, one, two, two],
            out_specs=[pl.BlockSpec((BLK, width), lambda g, *_: (0, g)), four, two, two],
            scratch_shapes=[
                pltpu.VMEM((NBLK * BLK, HEAD_DIM), jnp.bfloat16),
                pltpu.VMEM((NBLK * BLK, HEAD_DIM), jnp.bfloat16),
                pltpu.VMEM((NBLK * BLK, BLK), jnp.float32),
                pltpu.VMEM((NBLK * BLK, LANES), jnp.float32),
                pltpu.VMEM((NBLK * BLK, LANES), jnp.float32),
                pltpu.VMEM((NBLK, LANES), jnp.float32),
                pltpu.VMEM((HEAD_DIM, LANES), jnp.float32),
                pltpu.VMEM((2, NBLK * BLK, HEAD_DIM), jnp.float32),
            ],
        ),
        out_shape=[
            jax.ShapeDtypeStruct((BLK, GROUPS * width), jnp.bfloat16),
            jax.ShapeDtypeStruct((4, 2, BLK, columns), jnp.bfloat16),
            jax.ShapeDtypeStruct((2, 2, BLK, columns), jnp.bfloat16),
            jax.ShapeDtypeStruct((2, 2, BLK, columns), jnp.bfloat16),
        ],
        compiler_params=pltpu.CompilerParams(vmem_limit_bytes=40 * 1024 * 1024),
        cost_estimate=pl.CostEstimate(
            flops=GROUPS * RATIO * NBLK * 10 * BLK ** 3, bytes_accessed=GROUPS * 6 * BLK * width, transcendentals=0
        ),
    )(info, ends, queries, out_grad, own, from_left, from_right, from_y, from_x2, from_ylr)


def wide_sum(*terms):
    return functools.reduce(jnp.add, [term.astype(jnp.float32) for term in terms]).astype(jnp.bfloat16)


def per_device(queries, key_states, value_states, out_grad, node_end, block_list, block_count):
    place = lax.axis_index("ctx")
    info = jnp.concatenate([block_count[0, place][None], block_list[0, place], place[None].astype(jnp.int32)])
    ends = node_end.reshape(NBLK * BLK, 1)
    columns = GROUPS * HEAD_DIM
    query_parts, pair_parts = [], []
    for chunk in range(CHUNKS):
        span = slice(chunk * columns, (chunk + 1) * columns)
        own = jnp.concatenate([key_states[:, :, span], value_states[:, :, span]])
        from_left = send(own, right)
        from_right = send(own, left)
        from_y = send(own, up)
        from_x2 = send(jnp.stack([own, from_y]), across)
        from_ylr = send(jnp.stack([from_left, from_right]), up)
        dq, near, far, side = chunk_grads(
            chunk, info, ends, queries, out_grad, own, from_left, from_right, from_y, from_x2, from_ylr
        )
        query_parts.append(send_behind(dq, stay))
        side_in = send(side, down)
        far_in = send(far, across)
        terms = [
            send_behind(wide_sum(near[0], far_in[0]), stay),
            send_behind(wide_sum(near[1], side_in[0]), left),
            send_behind(wide_sum(near[2], side_in[1]), right),
            send_behind(wide_sum(near[3], far_in[1]), down),
        ]
        pair_parts.append(wide_sum(*terms))
    return (
        jnp.concatenate(query_parts, axis=1)[None],
        jnp.concatenate([part[0:1] for part in pair_parts], axis=2),
        jnp.concatenate([part[1:2] for part in pair_parts], axis=2),
    )


def solution(mesh):
    placed = (
        P("section", "ctx", None),
        P("section", "ctx", None),
        P("section", "ctx", None),
        P("section", "ctx", None),
        P("section", None),
        P("section", None, None),
        P("section", None),
    )
    return jax.shard_map(
        per_device,
        mesh=mesh,
        in_specs=placed,
        out_specs=(P("section", "ctx", None), P("section", "ctx", None), P("section", "ctx", None)),
        check_vma=False,
    )
```

time: 466 us -> 147 us (0.32); the launches traced: 458 us -> 144 us
  matrix products: 201 us -> 0 us
  waiting for transfers between devices: 187 us -> 66 us
  starting transfers between devices: 12.7 us -> 47.6 us
  local copies, waits for them, and re-layouts: 29.9 us -> 5.18 us
  Pallas kernels: 0 us -> 16.6 us
  between operations: 13.8 us -> 0.95 us
    dot_general x32 -> x0, matrix products: 167 us -> none  [the longest x8 58.1 us: head_block(): jnp.einsum('hqk,kd->qhd', score_grad, key_rows, preferred_element_type=jn...]
    reduce_scatter x1 -> x0, waiting for transfers between devices: 91.2 us -> none  [per_device(): summed = lax.psum_scatter(pair_acc, 'ctx', scatter_dimension=1, tiled=True)]
    all_gather x2 -> x0, waiting for transfers between devices: 88.2 us -> none  [the longest x1 45.2 us: per_device(): lax.all_gather(value_states, 'ctx', axis=1, tiled=True)]
    ppermute x2 -> x24, waiting for transfers between devices: 6.7 us -> 66 us  [the longest x14 43 us: send(): return lax.ppermute(block, 'ctx', ctx_route(move))]
    ppermute x2 -> x24, starting transfers between devices: 12.6 us -> 47.6 us  [the longest x14 32.8 us: send(): return lax.ppermute(block, 'ctx', ctx_route(move))]
    sub x8 -> x0, matrix products: 34 us -> none  [head_block(): exponent = jnp.exp(scores - row_max)]
    pallas_call x0 -> x2, Pallas kernels: none -> 16.6 us  [chunk_grads(): pl.pallas_call(grads_kernel, grid_spec=pltpu.PrefetchScalarGridSpec(num_s...]
    dynamic_slice x24 -> x1, local copies, waits for them, and re-layouts: 11.2 us -> 0.59 us  [per_device(): block_count[0, place][None]]
  transfers between devices with their start and end apart: 5 -> 24, of which waited for: 4 -> 7; matrix products, arithmetic and copies ran while one was open for 1% -> 5% of each run, Pallas kernels for 0% -> 11%
where the time goes in v1:
time: 147 us; the launch traced here: 144 us
  waiting for transfers between devices  66 us (45%)
  starting transfers between devices  47.6 us (32%)
  Pallas kernels  16.6 us (11%)
  other arithmetic  8.04 us (5%)
  local copies, waits for them, and re-layouts  5.18 us (4%)
    ppermute x14, waiting for transfers between devices, send(): return lax.ppermute(block, 'ctx', ctx_route(move))  43 us
    ppermute x14, starting transfers between devices, send(): return lax.ppermute(block, 'ctx', ctx_route(move))  32.8 us
    ppermute x10, waiting for transfers between devices, send_behind(): return lax.ppermute(block, ('section', 'ctx'), route)  23 us
    pallas_call x2, Pallas kernels, chunk_grads(): pl.pallas_call(grads_kernel, grid_spec=pltpu.PrefetchScalarGridSpec(num_s...  16.6 us
    ppermute x10, starting transfers between devices, send_behind(): return lax.ppermute(block, ('section', 'ctx'), route)  14.8 us
    unnamed x10, local copies, waits for them, and re-layouts  3.2 us
  transfers between devices with their start and end apart: 24, of which 7 were waited for; matrix products, arithmetic and copies ran while one was open for 5% of the time, Pallas kernels for 11%

profile of v1, /device:TPU:2, one launch (start us, length us, event | category | flops | bytes accessed | tf_op | source)
XLA Modules:
  0.0 144.4 jit_solution(3306099062714922251)
XLA Ops:
  1.8 1.6 %collective-permute-start = (bf16[2,128,512]{2,1,0:T(8,128)(2,1)S(1)}, bf16[2,128,512]{2,1,0:T(8,128)(2,1)S(1)}, u32[]{:S(2)}, u32[]{:S(2)}) collective-permute-start(bf16[2,128,512]{2,1,0:T(8,128)(2,1)S(1)} %get-tuple-element.36.own_ref), channel_id=1, source_target_pairs={{0,1},{1,2},{2,3},{3,0},{4,5},{5,6},{6,7},{7,4},{8,9},{9,10},{10,1... | collective-permute-start | bytes 786440 | tf_op jit(solution)/shard_map/ppermute | solution.py:61
  4.3 3.1 %collective-permute-start.2 = (bf16[2,128,512]{2,1,0:T(8,128)(2,1)S(1)}, bf16[2,128,512]{2,1,0:T(8,128)(2,1)S(1)}, u32[]{:S(2)}, u32[]{:S(2)}) collective-permute-start(bf16[2,128,512]{2,1,0:T(8,128)(2,1)S(1)} %get-tuple-element.36.own_ref), channel_id=1, source_target_pairs={{0,4},{1,5},{2,6},{3,7},{8,12},{9,13},{10,14},{11,15},{16,20},{17,... | collective-permute-start | bytes 786440 | tf_op jit(solution)/shard_map/ppermute | solution.py:61
  7.5 1.6 %collective-permute-start.6 = (bf16[2,128,512]{2,1,0:T(8,128)(2,1)S(1)}, bf16[2,128,512]{2,1,0:T(8,128)(2,1)S(1)}, u32[]{:S(2)}, u32[]{:S(2)}) collective-permute-start(bf16[2,128,512]{2,1,0:T(8,128)(2,1)S(1)} %get-tuple-element.42.own_ref), channel_id=1, source_target_pairs={{0,1},{1,2},{2,3},{3,0},{4,5},{5,6},{6,7},{7,4},{8,9},{9,10},{10,1... | collective-permute-start | bytes 786440 | tf_op jit(solution)/shard_map/ppermute | solution.py:61
  12.8 4.2 %collective-permute-start.4 = (bf16[2,2,128,512]{3,2,1,0:T(8,128)(2,1)}, bf16[2,2,128,512]{3,2,1,0:T(8,128)(2,1)S(1)}, u32[]{:S(2)}, u32[]{:S(2)}) collective-permute-start(bf16[2,2,128,512]{3,2,1,0:T(8,128)(2,1)} %pad_maximum_fusion.1), channel_id=1, source_target_pairs={{0,4},{1,5},{2,6},{3,7},{8,12},{9,13},{10,14},{11,15},{16,20},{17,... | collective-permute-start | bytes 1572872 | tf_op jit(solution)/shard_map/ppermute | solution.py:61
  17.8 2.3 %collective-permute-start.3 = (bf16[2,2,128,512]{3,2,1,0:T(8,128)(2,1)}, bf16[2,2,128,512]{3,2,1,0:T(8,128)(2,1)}, u32[]{:S(2)}, u32[]{:S(2)}) collective-permute-start(bf16[2,2,128,512]{3,2,1,0:T(8,128)(2,1)} %pad_maximum_fusion), channel_id=1, source_target_pairs={{0,2},{1,3},{2,0},{3,1},{4,6},{5,7},{6,4},{7,5},{8,10},{9,11},{10,... | collective-permute-start | bytes 1572872 | tf_op jit(solution)/shard_map/ppermute | solution.py:61
  20.2 1.3 collective-permute-start.8
  22.9 2.1 %collective-permute-start.10 = (bf16[2,2,128,512]{3,2,1,0:T(8,128)(2,1)}, bf16[2,2,128,512]{3,2,1,0:T(8,128)(2,1)}, u32[]{:S(2)}, u32[]{:S(2)}) collective-permute-start(bf16[2,2,128,512]{3,2,1,0:T(8,128)(2,1)} %pad_maximum_fusion.3), channel_id=1, source_target_pairs={{0,4},{1,5},{2,6},{3,7},{8,12},{9,13},{10,14},{11,15},{16,20},{17,... | collective-permute-start | bytes 1572872 | tf_op jit(solution)/shard_map/ppermute | solution.py:61
  25.0 10.1 %collective-permute-done.8.y_ref = bf16[2,128,512]{2,1,0:T(8,128)(2,1)S(1)} collective-permute-done((bf16[2,128,512]{2,1,0:T(8,128)(2,1)S(1)}, bf16[2,128,512]{2,1,0:T(8,128)(2,1)S(1)}, u32[]{:S(2)}, u32[]{:S(2)}) %collective-permute-start.8) | collective-permute-done | bytes 262176 | tf_op jit(solution)/shard_map/ppermute | solution.py:61
  36.0 2.3 %collective-permute-start.9 = (bf16[2,2,128,512]{3,2,1,0:T(8,128)(2,1)}, bf16[2,2,128,512]{3,2,1,0:T(8,128)(2,1)}, u32[]{:S(2)}, u32[]{:S(2)}) collective-permute-start(bf16[2,2,128,512]{3,2,1,0:T(8,128)(2,1)} %pad_maximum_fusion.2), channel_id=1, source_target_pairs={{0,2},{1,3},{2,0},{3,1},{4,6},{5,7},{6,4},{7,5},{8,10},{9,11},{10,... | collective-permute-start | bytes 1572872 | tf_op jit(solution)/shard_map/ppermute | solution.py:61
  39.3 1.6 %copy-done.1 = bf16[1,128,8192]{2,1,0:T(8,128)(2,1)S(1)} copy-done((bf16[1,128,8192]{2,1,0:T(8,128)(2,1)S(1)}, bf16[1,128,8192]{2,1,0:T(8,128)(2,1)}, u32[]{:S(2)}) %copy-start.1) | copy-done | bytes 2097176
  40.9 1.6 %copy-done.2 = bf16[1,128,8192]{2,1,0:T(8,128)(2,1)S(1)} copy-done((bf16[1,128,8192]{2,1,0:T(8,128)(2,1)S(1)}, bf16[1,128,8192]{2,1,0:T(8,128)(2,1)}, u32[]{:S(2)}) %copy-start.2) | copy-done | bytes 2097176
  42.5 8.3 %shard_map.94 = (bf16[128,4096]{1,0:T(8,128)(2,1)S(1)}, bf16[4,2,128,512]{3,2,1,0:T(8,128)(2,1)S(1)}, bf16[2,2,128,512]{3,2,1,0:T(8,128)(2,1)S(1)}, bf16[2,2,128,512]{3,2,1,0:T(8,128)(2,1)S(1)}) custom-call(s32[10]{0:T(128)S(1)} %pad_add_fusion.info, s32[1024,1]{1,0:T(8,128)S(1)} %copy.10.ends_ref, bf16[1,128,8192]{2,1,0:T(8,128)(2,1)S(1)} %copy-done.1, ...), custom_call_target="tpu_custom_call" | custom-call | flops 5368709120 | bytes 3145728 | tf_op jit(solution)/shard_map/pallas_call | solution.py:210
  50.8 5.8 %collective-permute-start.12 = (bf16[2,2,128,512]{3,2,1,0:T(8,128)(2,1)S(1)}, bf16[2,2,128,512]{3,2,1,0:T(8,128)(2,1)S(1)}, u32[]{:S(2)}, u32[]{:S(2)}) collective-permute-start(bf16[2,2,128,512]{3,2,1,0:T(8,128)(2,1)S(1)} %get-tuple-element.14), channel_id=1, source_target_pairs={{0,2},{1,3},{2,0},{3,1},{4,6},{5,7},{6,4},{7,5},{8,10},{9,11},{10,... | collective-permute-start | bytes 1572872 | tf_op jit(solution)/shard_map/ppermute | solution.py:61
  56.5 1.3 collective-permute-start.14
  57.8 8.3 %shard_map.95 = (bf16[128,4096]{1,0:T(8,128)(2,1)S(1)}, bf16[4,2,128,512]{3,2,1,0:T(8,128)(2,1)S(1)}, bf16[2,2,128,512]{3,2,1,0:T(8,128)(2,1)S(1)}, bf16[2,2,128,512]{3,2,1,0:T(8,128)(2,1)S(1)}) custom-call(s32[10]{0:T(128)S(1)} %pad_add_fusion.info, s32[1024,1]{1,0:T(8,128)S(1)} %copy.10.ends_ref, bf16[1,128,8192]{2,1,0:T(8,128)(2,1)S(1)} %copy-done.1, ...), custom_call_target="tpu_custom_call" | custom-call | flops 5368709120 | bytes 3145728 | tf_op jit(solution)/shard_map/pallas_call | solution.py:210
  66.1 4.6 %collective-permute-start.18 = (bf16[2,2,128,512]{3,2,1,0:T(8,128)(2,1)S(1)}, bf16[2,2,128,512]{3,2,1,0:T(8,128)(2,1)S(1)}, u32[]{:S(2)}, u32[]{:S(2)}) collective-permute-start(bf16[2,2,128,512]{3,2,1,0:T(8,128)(2,1)S(1)} %get-tuple-element.17), channel_id=1, source_target_pairs={{0,2},{1,3},{2,0},{3,1},{4,6},{5,7},{6,4},{7,5},{8,10},{9,11},{10,... | collective-permute-start | bytes 1572872 | tf_op jit(solution)/shard_map/ppermute | solution.py:61
  72.0 8.5 %collective-permute-done.14 = bf16[2,2,128,512]{3,2,1,0:T(8,128)(2,1)S(1)} collective-permute-done((bf16[2,2,128,512]{3,2,1,0:T(8,128)(2,1)S(1)}, bf16[2,2,128,512]{3,2,1,0:T(8,128)(2,1)S(1)}, u32[]{:S(2)}, u32[]{:S(2)}) %collective-permute-start.14) | collective-permute-done | bytes 524320 | tf_op jit(solution)/shard_map/ppermute | solution.py:61
  81.9 1.3 collective-permute-start.17
  83.2 22.0 %collective-permute-done.20 = bf16[2,2,128,512]{3,2,1,0:T(8,128)(2,1)S(1)} collective-permute-done((bf16[2,2,128,512]{3,2,1,0:T(8,128)(2,1)S(1)}, bf16[2,2,128,512]{3,2,1,0:T(8,128)(2,1)S(1)}, u32[]{:S(2)}, u32[]{:S(2)}) %collective-permute-start.20) | collective-permute-done | bytes 524320 | tf_op jit(solution)/shard_map/ppermute | solution.py:61
  106.0 10.9 %collective-permute-start.22 = (bf16[2,128,512]{2,1,0:T(8,128)(2,1)S(1)}, bf16[2,128,512]{2,1,0:T(8,128)(2,1)S(1)}, u32[]{:S(2)}, u32[]{:S(2)}) collective-permute-start(bf16[2,128,512]{2,1,0:T(8,128)(2,1)S(1)} %get-tuple-element.29), channel_id=1, source_target_pairs={{0,249},{1,250},{2,251},{3,248},{4,253},{5,254},{6,255},{7,252},{8... | collective-permute-start | bytes 786440 | tf_op jit(solution)/shard_map/ppermute | solution.py:70
  116.8 1.3 collective-permute-start.23
  118.3 20.1 %collective-permute-done.21 = bf16[2,128,512]{2,1,0:T(8,128)(2,1)S(1)} collective-permute-done((bf16[2,128,512]{2,1,0:T(8,128)(2,1)S(1)}, bf16[2,128,512]{2,1,0:T(8,128)(2,1)S(1)}, u32[]{:S(2)}, u32[]{:S(2)}) %collective-permute-start.21) | collective-permute-done | bytes 262176 | tf_op jit(solution)/shard_map/ppermute | solution.py:70
  138.4 2.8 %collective-permute-done.22 = bf16[2,128,512]{2,1,0:T(8,128)(2,1)S(1)} collective-permute-done((bf16[2,128,512]{2,1,0:T(8,128)(2,1)S(1)}, bf16[2,128,512]{2,1,0:T(8,128)(2,1)S(1)}, u32[]{:S(2)}, u32[]{:S(2)}) %collective-permute-start.22) | collective-permute-done | bytes 262176 | tf_op jit(solution)/shard_map/ppermute | solution.py:70
  142.9 1.5 %maximum_bitcast_fusion = bf16[1,128,8192]{2,1,0:T(8,128)(2,1)} fusion(bf16[128,4096]{1,0:T(8,128)(2,1)S(1)} %collective-permute-done.11, bf16[128,4096]{1,0:T(8,128)(2,1)S(1)} %collective-permute-done.5), kind=kLoop, calls=%fused_computation | loop fusion | flops 4194304 | bytes 4194304 | tf_op jit(solution)/shard_map/broadcast_in_dim | solution.py:273
  (56 shorter events, 15.0 us)
Async XLA Ops:
  1.8 8.9 %collective-permute-start = (bf16[2,128,512]{2,1,0:T(8,128)(2,1)S(1)}, bf16[2,128,512]{2,1,0:T(8,128)(2,1)S(1)}, u32[]{:S(2)}, u32[]{:S(2)}) collective-permute-start(bf16[2,128,512]{2,1,0:T(8,128)(2,1)S(1)} %get-tuple-element.36.own_ref), channel_id=1, source_target_pairs={{0,1},{1,2},{2,3},{3,0},{4,5},{5,6},{6,7},{7,4},{8,9},{9,10},{10,1... | collective-permute-start | bytes 786440 | tf_op jit(solution)/shard_map/ppermute | solution.py:61
  3.4 8.5 %collective-permute-start.1 = (bf16[2,128,512]{2,1,0:T(8,128)(2,1)S(1)}, bf16[2,128,512]{2,1,0:T(8,128)(2,1)S(1)}, u32[]{:S(2)}, u32[]{:S(2)}) collective-permute-start(bf16[2,128,512]{2,1,0:T(8,128)(2,1)S(1)} %get-tuple-element.36.own_ref), channel_id=1, source_target_pairs={{0,3},{1,0},{2,1},{3,2},{4,7},{5,4},{6,5},{7,6},{8,11},{9,8},{10,9... | collective-permute-start | bytes 786440 | tf_op jit(solution)/shard_map/ppermute | solution.py:61
  4.3 12.7 %collective-permute-start.2 = (bf16[2,128,512]{2,1,0:T(8,128)(2,1)S(1)}, bf16[2,128,512]{2,1,0:T(8,128)(2,1)S(1)}, u32[]{:S(2)}, u32[]{:S(2)}) collective-permute-start(bf16[2,128,512]{2,1,0:T(8,128)(2,1)S(1)} %get-tuple-element.36.own_ref), channel_id=1, source_target_pairs={{0,4},{1,5},{2,6},{3,7},{8,12},{9,13},{10,14},{11,15},{16,20},{17,... | collective-permute-start | bytes 786440 | tf_op jit(solution)/shard_map/ppermute | solution.py:61
  7.5 14.6 %collective-permute-start.6 = (bf16[2,128,512]{2,1,0:T(8,128)(2,1)S(1)}, bf16[2,128,512]{2,1,0:T(8,128)(2,1)S(1)}, u32[]{:S(2)}, u32[]{:S(2)}) collective-permute-start(bf16[2,128,512]{2,1,0:T(8,128)(2,1)S(1)} %get-tuple-element.42.own_ref), channel_id=1, source_target_pairs={{0,1},{1,2},{2,3},{3,0},{4,5},{5,6},{6,7},{7,4},{8,9},{9,10},{10,1... | collective-permute-start | bytes 786440 | tf_op jit(solution)/shard_map/ppermute | solution.py:61
  9.0 13.0 %collective-permute-start.7 = (bf16[2,128,512]{2,1,0:T(8,128)(2,1)S(1)}, bf16[2,128,512]{2,1,0:T(8,128)(2,1)S(1)}, u32[]{:S(2)}, u32[]{:S(2)}) collective-permute-start(bf16[2,128,512]{2,1,0:T(8,128)(2,1)S(1)} %get-tuple-element.42.own_ref), channel_id=1, source_target_pairs={{0,3},{1,0},{2,1},{3,2},{4,7},{5,4},{6,5},{7,6},{8,11},{9,8},{10,9... | collective-permute-start | bytes 786440 | tf_op jit(solution)/shard_map/ppermute | solution.py:61
  12.8 26.5 %collective-permute-start.4 = (bf16[2,2,128,512]{3,2,1,0:T(8,128)(2,1)}, bf16[2,2,128,512]{3,2,1,0:T(8,128)(2,1)S(1)}, u32[]{:S(2)}, u32[]{:S(2)}) collective-permute-start(bf16[2,2,128,512]{3,2,1,0:T(8,128)(2,1)} %pad_maximum_fusion.1), channel_id=1, source_target_pairs={{0,4},{1,5},{2,6},{3,7},{8,12},{9,13},{10,14},{11,15},{16,20},{17,... | collective-permute-start | bytes 1572872 | tf_op jit(solution)/shard_map/ppermute | solution.py:61
  17.8 21.4 %collective-permute-start.3 = (bf16[2,2,128,512]{3,2,1,0:T(8,128)(2,1)}, bf16[2,2,128,512]{3,2,1,0:T(8,128)(2,1)}, u32[]{:S(2)}, u32[]{:S(2)}) collective-permute-start(bf16[2,2,128,512]{3,2,1,0:T(8,128)(2,1)} %pad_maximum_fusion), channel_id=1, source_target_pairs={{0,2},{1,3},{2,0},{3,1},{4,6},{5,7},{6,4},{7,5},{8,10},{9,11},{10,... | collective-permute-start | bytes 1572872 | tf_op jit(solution)/shard_map/ppermute | solution.py:61
  20.2 15.0 %collective-permute-start.8 = (bf16[2,128,512]{2,1,0:T(8,128)(2,1)S(1)}, bf16[2,128,512]{2,1,0:T(8,128)(2,1)S(1)}, u32[]{:S(2)}, u32[]{:S(2)}) collective-permute-start(bf16[2,128,512]{2,1,0:T(8,128)(2,1)S(1)} %get-tuple-element.42.own_ref), channel_id=1, source_target_pairs={{0,4},{1,5},{2,6},{3,7},{8,12},{9,13},{10,14},{11,15},{16,20},{17,... | collective-permute-start | bytes 786440 | tf_op jit(solution)/shard_map/ppermute | solution.py:61
  22.9 34.9 %collective-permute-start.10 = (bf16[2,2,128,512]{3,2,1,0:T(8,128)(2,1)}, bf16[2,2,128,512]{3,2,1,0:T(8,128)(2,1)}, u32[]{:S(2)}, u32[]{:S(2)}) collective-permute-start(bf16[2,2,128,512]{3,2,1,0:T(8,128)(2,1)} %pad_maximum_fusion.3), channel_id=1, source_target_pairs={{0,4},{1,5},{2,6},{3,7},{8,12},{9,13},{10,14},{11,15},{16,20},{17,... | collective-permute-start | bytes 1572872 | tf_op jit(solution)/shard_map/ppermute | solution.py:61
  36.0 21.8 %collective-permute-start.9 = (bf16[2,2,128,512]{3,2,1,0:T(8,128)(2,1)}, bf16[2,2,128,512]{3,2,1,0:T(8,128)(2,1)}, u32[]{:S(2)}, u32[]{:S(2)}) collective-permute-start(bf16[2,2,128,512]{3,2,1,0:T(8,128)(2,1)} %pad_maximum_fusion.2), channel_id=1, source_target_pairs={{0,2},{1,3},{2,0},{3,1},{4,6},{5,7},{6,4},{7,5},{8,10},{9,11},{10,... | collective-permute-start | bytes 1572872 | tf_op jit(solution)/shard_map/ppermute | solution.py:61
  50.8 21.3 %collective-permute-start.12 = (bf16[2,2,128,512]{3,2,1,0:T(8,128)(2,1)S(1)}, bf16[2,2,128,512]{3,2,1,0:T(8,128)(2,1)S(1)}, u32[]{:S(2)}, u32[]{:S(2)}) collective-permute-start(bf16[2,2,128,512]{3,2,1,0:T(8,128)(2,1)S(1)} %get-tuple-element.14), channel_id=1, source_target_pairs={{0,2},{1,3},{2,0},{3,1},{4,6},{5,7},{6,4},{7,5},{8,10},{9,11},{10,... | collective-permute-start | bytes 1572872 | tf_op jit(solution)/shard_map/ppermute | solution.py:61
  56.5 24.1 %collective-permute-start.14 = (bf16[2,2,128,512]{3,2,1,0:T(8,128)(2,1)S(1)}, bf16[2,2,128,512]{3,2,1,0:T(8,128)(2,1)S(1)}, u32[]{:S(2)}, u32[]{:S(2)}) collective-permute-start(bf16[2,2,128,512]{3,2,1,0:T(8,128)(2,1)S(1)} %get-tuple-element.15), channel_id=1, source_target_pairs={{4,0},{5,1},{6,2},{7,3},{12,8},{13,9},{14,10},{15,11},{20,16},{21,... | collective-permute-start | bytes 1572872 | tf_op jit(solution)/shard_map/ppermute | solution.py:61
  66.1 15.8 %collective-permute-start.18 = (bf16[2,2,128,512]{3,2,1,0:T(8,128)(2,1)S(1)}, bf16[2,2,128,512]{3,2,1,0:T(8,128)(2,1)S(1)}, u32[]{:S(2)}, u32[]{:S(2)}) collective-permute-start(bf16[2,2,128,512]{3,2,1,0:T(8,128)(2,1)S(1)} %get-tuple-element.17), channel_id=1, source_target_pairs={{0,2},{1,3},{2,0},{3,1},{4,6},{5,7},{6,4},{7,5},{8,10},{9,11},{10,... | collective-permute-start | bytes 1572872 | tf_op jit(solution)/shard_map/ppermute | solution.py:61
  70.7 34.5 %collective-permute-start.20 = (bf16[2,2,128,512]{3,2,1,0:T(8,128)(2,1)S(1)}, bf16[2,2,128,512]{3,2,1,0:T(8,128)(2,1)S(1)}, u32[]{:S(2)}, u32[]{:S(2)}) collective-permute-start(bf16[2,2,128,512]{3,2,1,0:T(8,128)(2,1)S(1)} %get-tuple-element.18), channel_id=1, source_target_pairs={{4,0},{5,1},{6,2},{7,3},{12,8},{13,9},{14,10},{15,11},{20,16},{21,... | collective-permute-start | bytes 1572872 | tf_op jit(solution)/shard_map/ppermute | solution.py:61
  80.9 24.7 %collective-permute-start.13 = (bf16[2,128,512]{2,1,0:T(8,128)(2,1)S(1)}, bf16[2,128,512]{2,1,0:T(8,128)(2,1)S(1)}, u32[]{:S(2)}, u32[]{:S(2)}) collective-permute-start(bf16[2,128,512]{2,1,0:T(8,128)(2,1)S(1)} %get-tuple-element.19), channel_id=1, source_target_pairs={{0,248},{1,249},{2,250},{3,251},{4,252},{5,253},{6,254},{7,255},{8... | collective-permute-start | bytes 786440 | tf_op jit(solution)/shard_map/ppermute | solution.py:70
  81.0 24.7 %collective-permute-start.15 = (bf16[2,128,512]{2,1,0:T(8,128)(2,1)S(1)}, bf16[2,128,512]{2,1,0:T(8,128)(2,1)S(1)}, u32[]{:S(2)}, u32[]{:S(2)}) collective-permute-start(bf16[2,128,512]{2,1,0:T(8,128)(2,1)S(1)} %get-tuple-element.28), channel_id=1, source_target_pairs={{0,251},{1,248},{2,249},{3,250},{4,255},{5,252},{6,253},{7,254},{8... | collective-permute-start | bytes 786440 | tf_op jit(solution)/shard_map/ppermute | solution.py:70
  81.1 24.8 %collective-permute-start.16 = (bf16[2,128,512]{2,1,0:T(8,128)(2,1)S(1)}, bf16[2,128,512]{2,1,0:T(8,128)(2,1)S(1)}, u32[]{:S(2)}, u32[]{:S(2)}) collective-permute-start(bf16[2,128,512]{2,1,0:T(8,128)(2,1)S(1)} %get-tuple-element.27), channel_id=1, source_target_pairs={{0,249},{1,250},{2,251},{3,248},{4,253},{5,254},{6,255},{7,252},{8... | collective-permute-start | bytes 786440 | tf_op jit(solution)/shard_map/ppermute | solution.py:70
  81.9 24.0 %collective-permute-start.17 = (bf16[2,128,512]{2,1,0:T(8,128)(2,1)S(1)}, bf16[2,128,512]{2,1,0:T(8,128)(2,1)S(1)}, u32[]{:S(2)}, u32[]{:S(2)}) collective-permute-start(bf16[2,128,512]{2,1,0:T(8,128)(2,1)S(1)} %get-tuple-element.20), channel_id=1, source_target_pairs={{4,248},{5,249},{6,250},{7,251},{12,0},{13,1},{14,2},{15,3},{20,8}... | collective-permute-start | bytes 786440 | tf_op jit(solution)/shard_map/ppermute | solution.py:70
  105.5 11.3 %collective-permute-start.19 = (bf16[2,128,512]{2,1,0:T(8,128)(2,1)S(1)}, bf16[2,128,512]{2,1,0:T(8,128)(2,1)S(1)}, u32[]{:S(2)}, u32[]{:S(2)}) collective-permute-start(bf16[2,128,512]{2,1,0:T(8,128)(2,1)S(1)} %get-tuple-element.23), channel_id=1, source_target_pairs={{0,248},{1,249},{2,250},{3,251},{4,252},{5,253},{6,254},{7,255},{8... | collective-permute-start | bytes 786440 | tf_op jit(solution)/shard_map/ppermute | solution.py:70
  105.6 37.2 %collective-permute-start.5 = (bf16[128,4096]{1,0:T(8,128)(2,1)S(1)}, bf16[128,4096]{1,0:T(8,128)(2,1)S(1)}, u32[]{:S(2)}, u32[]{:S(2)}) collective-permute-start(bf16[128,4096]{1,0:T(8,128)(2,1)S(1)} %get-tuple-element.11), channel_id=1, source_target_pairs={{0,248},{1,249},{2,250},{3,251},{4,252},{5,253},{6,254},{7,255},{8... | collective-permute-start | bytes 3145736 | tf_op jit(solution)/shard_map/ppermute | solution.py:70
  105.7 37.1 %collective-permute-start.11 = (bf16[128,4096]{1,0:T(8,128)(2,1)S(1)}, bf16[128,4096]{1,0:T(8,128)(2,1)S(1)}, u32[]{:S(2)}, u32[]{:S(2)}) collective-permute-start(bf16[128,4096]{1,0:T(8,128)(2,1)S(1)} %get-tuple-element.12), channel_id=1, source_target_pairs={{0,248},{1,249},{2,250},{3,251},{4,252},{5,253},{6,254},{7,255},{8... | collective-permute-start | bytes 3145736 | tf_op jit(solution)/shard_map/ppermute | solution.py:70
  105.9 32.6 %collective-permute-start.21 = (bf16[2,128,512]{2,1,0:T(8,128)(2,1)S(1)}, bf16[2,128,512]{2,1,0:T(8,128)(2,1)S(1)}, u32[]{:S(2)}, u32[]{:S(2)}) collective-permute-start(bf16[2,128,512]{2,1,0:T(8,128)(2,1)S(1)} %get-tuple-element.30), channel_id=1, source_target_pairs={{0,251},{1,248},{2,249},{3,250},{4,255},{5,252},{6,253},{7,254},{8... | collective-permute-start | bytes 786440 | tf_op jit(solution)/shard_map/ppermute | solution.py:70
  106.0 35.3 %collective-permute-start.22 = (bf16[2,128,512]{2,1,0:T(8,128)(2,1)S(1)}, bf16[2,128,512]{2,1,0:T(8,128)(2,1)S(1)}, u32[]{:S(2)}, u32[]{:S(2)}) collective-permute-start(bf16[2,128,512]{2,1,0:T(8,128)(2,1)S(1)} %get-tuple-element.29), channel_id=1, source_target_pairs={{0,249},{1,250},{2,251},{3,248},{4,253},{5,254},{6,255},{7,252},{8... | collective-permute-start | bytes 786440 | tf_op jit(solution)/shard_map/ppermute | solution.py:70
  116.8 24.4 %collective-permute-start.23 = (bf16[2,128,512]{2,1,0:T(8,128)(2,1)S(1)}, bf16[2,128,512]{2,1,0:T(8,128)(2,1)S(1)}, u32[]{:S(2)}, u32[]{:S(2)}) collective-permute-start(bf16[2,128,512]{2,1,0:T(8,128)(2,1)S(1)} %get-tuple-element.24), channel_id=1, source_target_pairs={{4,248},{5,249},{6,250},{7,251},{12,0},{13,1},{14,2},{15,3},{20,8}... | collective-permute-start | bytes 786440 | tf_op jit(solution)/shard_map/ppermute | solution.py:70
  (5 other events, 71.4 us)

commit v2 on v1

--- a/solution.py
+++ b/solution.py
@@ -17,8 +17,7 @@
 LANES = RATIO * BLK
 HALF = 2 * BLK
 RING = 4
-CHUNKS = 2
-GROUPS = KV_HEADS // CHUNKS
+SPLIT = (3, 3, 2)
 SCALE = 1.0 / math.sqrt(HEAD_DIM)
 LOG2E = math.log2(math.e)
 LOWEST = -3.0e38
@@ -53,30 +52,22 @@
     return (0, x) if y == 1 else None
 
 
-def stay(y, x):
-    return (y, x)
-
-
 def send(block, move):
     return lax.ppermute(block, "ctx", ctx_route(move))
 
 
-def send_behind(block, move):
+def to_previous_section(block):
     sections = lax.axis_size("section")
-    route = []
-    for section in range(sections):
-        for source, target in ctx_route(move):
-            route.append((section * NBLK + source, ((section - 1) % sections) * NBLK + target))
-    return lax.ppermute(block, ("section", "ctx"), route)
+    return lax.ppermute(block, "section", [((s + 1) % sections, s) for s in range(sections)])
 
 
 def nt_dot(a, b):
     return lax.dot_general(a, b, (((1,), (1,)), ((), ())), preferred_element_type=jnp.float32)
 
 
-def grads_kernel(info, ends_ref, q_ref, g_ref, own_ref, left_ref, right_ref, y_ref, x2_ref, ylr_ref,
-                 dq_ref, near_ref, far_ref, side_ref,
-                 keys, values, bias, weights, wgrads, tops, dq_acc, pair_acc):
+def grads_kernel(by_block, info, ends_ref, q_ref, g_ref, own_ref, left_ref, right_ref, y_ref, x2_ref, ylr_ref,
+                 dq_ref, *refs):
+    part_refs, (keys, values, bias, weights, wgrads, tops, dq_acc, pair_acc) = refs[:-8], refs[-8:]
     count = info[0]
     row_place = info[9]
     y = row_place // RING
@@ -94,7 +85,7 @@
         for entry in range(NBLK):
             block = info[1 + entry]
             column = block * BLK + inner
-            ends = ends_ref[pl.ds(pl.multiple_of(block * BLK, BLK), BLK), :]
+            ends = jnp.broadcast_to(ends_ref[pl.ds(block, 1), :], (BLK, BLK)).T
             good = (column <= row) & (row < ends) & (entry < count)
             bias[pl.ds(entry * BLK, BLK), :] = jnp.where(good, 0.0, -jnp.inf)
 
@@ -184,36 +175,34 @@
     for head in range(RATIO):
         lanes = slice(head * BLK, (head + 1) * BLK)
         dq_ref[:, lanes] = dq_acc[:, lanes].T.astype(jnp.bfloat16)
-    outs = (
-        (near_ref, (0,), slots[0][2]),
-        (near_ref, (1,), slots[1][2]),
-        (near_ref, (2,), slots[2][2]),
-        (near_ref, (3,), slots[3][2]),
-        (far_ref, (0,), slots[4][2]),
-        (far_ref, (1,), slots[5][2]),
-        (side_ref, (0,), slots[6][2]),
-        (side_ref, (1,), slots[7][2]),
-    )
+    if by_block:
+        outs = [(part_refs[0], (block,), block) for block in range(NBLK)]
+    else:
+        stay_ref, to_left_ref, to_right_ref, far_ref = part_refs
+        leads = [(stay_ref, 0), (to_left_ref, 0), (to_right_ref, 0), (stay_ref, 1)]
+        leads += [(far_ref, 0), (far_ref, 1), (to_left_ref, 1), (to_right_ref, 1)]
+        outs = [(ref, (at,), slot[2]) for (ref, at), slot in zip(leads, slots)]
     for ref, lead, place in outs:
         rows = pl.ds(pl.multiple_of(place * BLK, BLK), BLK)
         for which in range(2):
             ref[(*lead, which)] = pair_acc[which, rows, :].astype(ref.dtype)
 
 
-def chunk_grads(chunk, info, ends, queries, out_grad, own, from_left, from_right, from_y, from_x2, from_ylr):
+def chunk_grads(by_block, at, base, groups, info, ends, queries, out_grad, own, from_left, from_right, from_y, from_x2, from_ylr):
     width = LANES
-    wide = pl.BlockSpec((1, BLK, width), lambda g, *_: (0, 0, chunk * GROUPS + g))
-    one = pl.BlockSpec((2, BLK, HEAD_DIM), lambda g, *_: (0, 0, g))
-    two = pl.BlockSpec((2, 2, BLK, HEAD_DIM), lambda g, *_: (0, 0, 0, g))
-    four = pl.BlockSpec((4, 2, BLK, HEAD_DIM), lambda g, *_: (0, 0, 0, g))
-    columns = GROUPS * HEAD_DIM
+    wide = pl.BlockSpec((1, BLK, width), lambda g, *_: (0, 0, base + at + g))
+    one = pl.BlockSpec((2, BLK, HEAD_DIM), lambda g, *_: (0, 0, at + g))
+    two = pl.BlockSpec((2, 2, BLK, HEAD_DIM), lambda g, *_: (0, 0, 0, at + g))
+    outs = (NBLK,) if by_block else (2, 2, 2, 2)
+    columns = groups * HEAD_DIM
     return pl.pallas_call(
-        grads_kernel,
+        functools.partial(grads_kernel, by_block),
         grid_spec=pltpu.PrefetchScalarGridSpec(
             num_scalar_prefetch=1,
-            grid=(GROUPS,),
-            in_specs=[pl.BlockSpec((NBLK * BLK, 1), lambda g, *_: (0, 0)), wide, wide, one, one, one, one, two, two],
-            out_specs=[pl.BlockSpec((BLK, width), lambda g, *_: (0, g)), four, two, two],
+            grid=(groups,),
+            in_specs=[pl.BlockSpec((NBLK, BLK), lambda g, *_: (0, 0)), wide, wide, one, one, one, one, two, two],
+            out_specs=[pl.BlockSpec((BLK, width), lambda g, *_: (0, g))]
+            + [pl.BlockSpec((n, 2, BLK, HEAD_DIM), lambda g, *_: (0, 0, 0, g)) for n in outs],
             scratch_shapes=[
                 pltpu.VMEM((NBLK * BLK, HEAD_DIM), jnp.bfloat16),
                 pltpu.VMEM((NBLK * BLK, HEAD_DIM), jnp.bfloat16),
@@ -226,54 +215,79 @@
             ],
         ),
         out_shape=[
-            jax.ShapeDtypeStruct((BLK, GROUPS * width), jnp.bfloat16),
-            jax.ShapeDtypeStruct((4, 2, BLK, columns), jnp.bfloat16),
-            jax.ShapeDtypeStruct((2, 2, BLK, columns), jnp.bfloat16),
-            jax.ShapeDtypeStruct((2, 2, BLK, columns), jnp.bfloat16),
-        ],
+            jax.ShapeDtypeStruct((BLK, groups * width), jnp.bfloat16),
+        ]
+        + [jax.ShapeDtypeStruct((n, 2, BLK, columns), jnp.bfloat16) for n in outs],
         compiler_params=pltpu.CompilerParams(vmem_limit_bytes=40 * 1024 * 1024),
         cost_estimate=pl.CostEstimate(
-            flops=GROUPS * RATIO * NBLK * 10 * BLK ** 3, bytes_accessed=GROUPS * 6 * BLK * width, transcendentals=0
+            flops=groups * RATIO * NBLK * 50 * BLK ** 3, bytes_accessed=groups * 6 * BLK * width, transcendentals=0
         ),
     )(info, ends, queries, out_grad, own, from_left, from_right, from_y, from_x2, from_ylr)
 
 
 def wide_sum(*terms):
     return functools.reduce(jnp.add, [term.astype(jnp.float32) for term in terms]).astype(jnp.bfloat16)
+
+
+def after(value, *others):
+    return lax.optimization_barrier((value, *others))[0]
 
 
 def per_device(queries, key_states, value_states, out_grad, node_end, block_list, block_count):
     place = lax.axis_index("ctx")
     info = jnp.concatenate([block_count[0, place][None], block_list[0, place], place[None].astype(jnp.int32)])
-    ends = node_end.reshape(NBLK * BLK, 1)
-    columns = GROUPS * HEAD_DIM
-    query_parts, pair_parts = [], []
-    for chunk in range(CHUNKS):
-        span = slice(chunk * columns, (chunk + 1) * columns)
-        own = jnp.concatenate([key_states[:, :, span], value_states[:, :, span]])
-        from_left = send(own, right)
-        from_right = send(own, left)
+    ends = node_end.reshape(NBLK, BLK)
+    firsts = [sum(SPLIT[:chunk]) for chunk in range(4)]
+
+    def mine(first, end):
+        span = slice(firsts[first] * HEAD_DIM, firsts[end] * HEAD_DIM)
+        return jnp.concatenate([key_states[:, :, span], value_states[:, :, span]])
+
+    def near_round(own):
         from_y = send(own, up)
-        from_x2 = send(jnp.stack([own, from_y]), across)
-        from_ylr = send(jnp.stack([from_left, from_right]), up)
-        dq, near, far, side = chunk_grads(
-            chunk, info, ends, queries, out_grad, own, from_left, from_right, from_y, from_x2, from_ylr
+        return send(own, right), send(own, left), from_y
+
+    def far_round(own, near):
+        sides = send(jnp.stack([near[0], near[1]]), up)
+        return send(jnp.stack([own, near[2]]), across), sides
+
+    def joined(*parts):
+        return jnp.concatenate(parts, axis=2)
+
+    def reduce_x(to_left, to_right, far):
+        return send(to_left, left), send(to_right, right), send(far, across)
+
+    def run(chunk, held, base, *gathered):
+        return chunk_grads(
+            False, firsts[chunk] - base, base, SPLIT[chunk], held, ends, queries, out_grad, *gathered
         )
-        query_parts.append(send_behind(dq, stay))
-        side_in = send(side, down)
-        far_in = send(far, across)
-        terms = [
-            send_behind(wide_sum(near[0], far_in[0]), stay),
-            send_behind(wide_sum(near[1], side_in[0]), left),
-            send_behind(wide_sum(near[2], side_in[1]), right),
-            send_behind(wide_sum(near[3], far_in[1]), down),
-        ]
-        pair_parts.append(wide_sum(*terms))
-    return (
-        jnp.concatenate(query_parts, axis=1)[None],
-        jnp.concatenate([part[0:1] for part in pair_parts], axis=2),
-        jnp.concatenate([part[1:2] for part in pair_parts], axis=2),
-    )
+
+    own0 = mine(0, 1)
+    near_round0 = near_round(own0)
+    far_round0 = far_round(own0, near_round0)
+    own12 = mine(1, 3)
+    near_round12 = near_round(own12)
+    far_round12 = far_round(own12, near_round12)
+    gathered12 = (own12, *near_round12, *far_round12)
+
+    dq0, stay0, *away0 = run(0, after(info, *near_round12), 0, own0, *near_round0, *far_round0)
+    moved0 = to_previous_section(dq0)
+    back0 = reduce_x(*away0)
+    dq1, stay1, *away1 = run(1, info, SPLIT[0], *gathered12)
+    moved1 = to_previous_section(dq1)
+    back1 = reduce_x(*away1)
+    dq2, stay2, *away2 = run(2, after(info, moved0, *back0), SPLIT[0], *gathered12)
+    back2 = reduce_x(*away2)
+    moved2 = to_previous_section(dq2)
+    sums0, sums1 = [
+        wide_sum(after(stay, stay2), *back) for stay, back in ((stay0, back0), (stay1, back1))
+    ]
+    down01 = send(joined(sums0[1], sums1[1]), down)
+    sums2 = wide_sum(stay2, *back2)
+    down2 = send(sums2[1], down)
+    home = joined(sums0[0], sums1[0], sums2[0])
+    pair = to_previous_section(wide_sum(home, joined(down01, down2)))
+    return (jnp.concatenate([moved0, moved1, moved2], axis=1)[None], pair[0:1], pair[1:2])
 
 
 def solution(mesh):

time: 147 us -> 129 us (0.88); the launches traced: 144 us -> 131 us
  waiting for transfers between devices: 66 us -> 19.6 us
  starting transfers between devices: 47.6 us -> 86 us
  other arithmetic: 8.04 us -> 3.23 us
    ppermute x14 -> x21, waiting for transfers between devices: 43 us -> 14.4 us  [send(): return lax.ppermute(block, 'ctx', ctx_route(move))]
    ppermute x14 -> x21, starting transfers between devices: 32.8 us -> 59.5 us  [send(): return lax.ppermute(block, 'ctx', ctx_route(move))]
    ppermute x10 -> x4, waiting for transfers between devices: 23 us -> 5.23 us  [to_previous_section(): lax.ppermute(block, 'section', [((s + 1) % sections, s) for s in range(se...]
    ppermute x10 -> x4, starting transfers between devices: 14.8 us -> 26.5 us  [to_previous_section(): lax.ppermute(block, 'section', [((s + 1) % sections, s) for s in range(se...]
    slice x3 -> x5, local copies, waits for them, and re-layouts: 1.17 us -> 4.51 us  [the longest x4 3.68 us: mine(): return jnp.concatenate([key_states[:, :, span], value_states[:, :, span]])]
    unnamed x10, local copies, waits for them, and re-layouts: 3.2 us -> 0.03 us
    another operation x6, other arithmetic: 3.45 us -> 0.33 us  [the longest x4 0.21 us: far_round(): return (send(jnp.stack([own, near[2]]), across), sides)]
    pallas_call x2 -> x3, Pallas kernels: 16.6 us -> 16.1 us  [chunk_grads(): pl.pallas_call(functools.partial(grads_kernel, by_block), grid_spec=pltpu...]
  transfers between devices with their start and end apart: 24 -> 25, of which waited for: 7 -> 6; matrix products, arithmetic and copies ran while one was open for 5% -> 4% of each run, Pallas kernels for 11% -> 12%
where the time goes in v2:
time: 129 us; the launch traced here: 131 us
  starting transfers between devices  86 us (67%)
  waiting for transfers between devices  19.6 us (15%)
  Pallas kernels  16.1 us (12%)
  local copies, waits for them, and re-layouts  5.23 us (4%)
  other arithmetic  3.23 us (3%)
    ppermute x21, starting transfers between devices, send(): return lax.ppermute(block, 'ctx', ctx_route(move))  59.5 us
    ppermute x4, starting transfers between devices, to_previous_section(): lax.ppermute(block, 'section', [((s + 1) % sections, s) for s in range(se...  26.5 us
    pallas_call x3, Pallas kernels, chunk_grads(): pl.pallas_call(functools.partial(grads_kernel, by_block), grid_spec=pltpu...  16.1 us
    ppermute x21, waiting for transfers between devices, send(): return lax.ppermute(block, 'ctx', ctx_route(move))  14.4 us
    ppermute x4, waiting for transfers between devices, to_previous_section(): lax.ppermute(block, 'section', [((s + 1) % sections, s) for s in range(se...  5.23 us
    slice x4, local copies, waits for them, and re-layouts, mine(): return jnp.concatenate([key_states[:, :, span], value_states[:, :, span]])  3.68 us
  transfers between devices with their start and end apart: 25, of which 6 were waited for; matrix products, arithmetic and copies ran while one was open for 4% of the time, Pallas kernels for 12%

profile of v2, /device:TPU:2, one launch (start us, length us, event | category | flops | bytes accessed | tf_op | source)
XLA Modules:
  0.0 131.2 jit_solution(6521153916897452684)
XLA Ops:
  2.5 1.6 %collective-permute-start.3 = (bf16[2,128,384]{2,1,0:T(8,128)(2,1)S(1)}, bf16[2,128,384]{2,1,0:T(8,128)(2,1)S(1)}, u32[]{:S(2)}, u32[]{:S(2)}) collective-permute-start(bf16[2,128,384]{2,1,0:T(8,128)(2,1)S(1)} %get-tuple-element.52.own_ref), channel_id=1, source_target_pairs={{0,1},{1,2},{2,3},{3,0},{4,5},{5,6},{6,7},{7,4},{8,9},{9,10},{10,1... | collective-permute-start | bytes 589832 | tf_op jit(solution)/shard_map/ppermute | solution.py:56
  5.0 3.1 %collective-permute-start.5 = (bf16[2,128,384]{2,1,0:T(8,128)(2,1)S(1)}, bf16[2,128,384]{2,1,0:T(8,128)(2,1)S(1)}, u32[]{:S(2)}, u32[]{:S(2)}) collective-permute-start(bf16[2,128,384]{2,1,0:T(8,128)(2,1)S(1)} %get-tuple-element.52.own_ref), channel_id=1, source_target_pairs={{0,4},{1,5},{2,6},{3,7},{8,12},{9,13},{10,14},{11,15},{16,20},{17,... | collective-permute-start | bytes 589832 | tf_op jit(solution)/shard_map/ppermute | solution.py:56
  10.1 1.6 %collective-permute-start = (bf16[2,128,640]{2,1,0:T(8,128)(2,1)S(1)}, bf16[2,128,640]{2,1,0:T(8,128)(2,1)S(1)}, u32[]{:S(2)}, u32[]{:S(2)}) collective-permute-start(bf16[2,128,640]{2,1,0:T(8,128)(2,1)S(1)} %get-tuple-element.48.own_ref), channel_id=1, source_target_pairs={{0,1},{1,2},{2,3},{3,0},{4,5},{5,6},{6,7},{7,4},{8,9},{9,10},{10,1... | collective-permute-start | bytes 983048 | tf_op jit(solution)/shard_map/ppermute | solution.py:56
  13.6 1.7 %collective-permute-start.7 = (bf16[2,2,128,384]{3,2,1,0:T(8,128)(2,1)S(1)}, bf16[2,2,128,384]{3,2,1,0:T(8,128)(2,1)S(1)}, u32[]{:S(2)}, u32[]{:S(2)}) collective-permute-start(bf16[2,2,128,384]{3,2,1,0:T(8,128)(2,1)S(1)} %pad_maximum_fusion.3), channel_id=1, source_target_pairs={{0,4},{1,5},{2,6},{3,7},{8,12},{9,13},{10,14},{11,15},{16,20},{17,... | collective-permute-start | bytes 1179656 | tf_op jit(solution)/shard_map/ppermute | solution.py:56
  15.3 2.2 %collective-permute-start.6 = (bf16[2,2,128,384]{3,2,1,0:T(8,128)(2,1)S(1)}, bf16[2,2,128,384]{3,2,1,0:T(8,128)(2,1)S(1)}, u32[]{:S(2)}, u32[]{:S(2)}) collective-permute-start(bf16[2,2,128,384]{3,2,1,0:T(8,128)(2,1)S(1)} %pad_maximum_fusion.2), channel_id=1, source_target_pairs={{0,2},{1,3},{2,0},{3,1},{4,6},{5,7},{6,4},{7,5},{8,10},{9,11},{10,... | collective-permute-start | bytes 1179656 | tf_op jit(solution)/shard_map/ppermute | solution.py:56
  19.5 2.2 %collective-permute-done.1.right_ref = bf16[2,128,640]{2,1,0:T(8,128)(2,1)S(1)} collective-permute-done((bf16[2,128,640]{2,1,0:T(8,128)(2,1)S(1)}, bf16[2,128,640]{2,1,0:T(8,128)(2,1)S(1)}, u32[]{:S(2)}, u32[]{:S(2)}) %collective-permute-start.1) | collective-permute-done | bytes 327712 | tf_op jit(solution)/shard_map/ppermute | solution.py:56
  21.7 4.4 %collective-permute-start.10 = (bf16[2,2,128,640]{3,2,1,0:T(8,128)(2,1)S(1)}, bf16[2,2,128,640]{3,2,1,0:T(8,128)(2,1)S(1)}, u32[]{:S(2)}, u32[]{:S(2)}) collective-permute-start(bf16[2,2,128,640]{3,2,1,0:T(8,128)(2,1)S(1)} %pad_maximum_fusion.1), channel_id=1, source_target_pairs={{0,4},{1,5},{2,6},{3,7},{8,12},{9,13},{10,14},{11,15},{16,20},{17,... | collective-permute-start | bytes 1966088 | tf_op jit(solution)/shard_map/ppermute | solution.py:56
  26.2 14.6 %collective-permute-start.9 = (bf16[2,2,128,640]{3,2,1,0:T(8,128)(2,1)S(1)}, bf16[2,2,128,640]{3,2,1,0:T(8,128)(2,1)S(1)}, u32[]{:S(2)}, u32[]{:S(2)}) collective-permute-start(bf16[2,2,128,640]{3,2,1,0:T(8,128)(2,1)S(1)} %pad_maximum_fusion), channel_id=1, source_target_pairs={{0,2},{1,3},{2,0},{3,1},{4,6},{5,7},{6,4},{7,5},{8,10},{9,11},{10,... | collective-permute-start | bytes 1966088 | tf_op jit(solution)/shard_map/ppermute | solution.py:56
  40.8 5.9 %shard_map.94 = (bf16[128,3072]{1,0:T(8,128)(2,1)S(1)}, bf16[2,2,128,384]{3,2,1,0:T(8,128)(2,1)S(1)}, bf16[2,2,128,384]{3,2,1,0:T(8,128)(2,1)S(1)}, bf16[2,2,128...) custom-call(s32[10]{0:T(128)S(1)} %pad_add_fusion.info, s32[8,128]{1,0:T(8,128)S(1)} %bitcast.35, ...), custom_call_target="tpu_custom_call" | custom-call | flops 20132659200 | bytes 2359296 | tf_op jit(solution)/shard_map/pallas_call | solution.py:198
  47.0 3.1 %collective-permute-start.13 = (bf16[2,2,128,384]{3,2,1,0:T(8,128)(2,1)S(1)}, bf16[2,2,128,384]{3,2,1,0:T(8,128)(2,1)S(1)}, u32[]{:S(2)}, u32[]{:S(2)}) collective-permute-start(bf16[2,2,128,384]{3,2,1,0:T(8,128)(2,1)S(1)} %get-tuple-element.26), channel_id=1, source_target_pairs={{0,1},{1,2},{2,3},{3,0},{4,5},{5,6},{6,7},{7,4},{8,9},{9,10},{10,1... | collective-permute-start | bytes 1179656 | tf_op jit(solution)/shard_map/ppermute | solution.py:56
  50.1 3.5 %collective-permute-start.14 = (bf16[2,2,128,384]{3,2,1,0:T(8,128)(2,1)S(1)}, bf16[2,2,128,384]{3,2,1,0:T(8,128)(2,1)S(1)}, u32[]{:S(2)}, u32[]{:S(2)}) collective-permute-start(bf16[2,2,128,384]{3,2,1,0:T(8,128)(2,1)S(1)} %get-tuple-element.27), channel_id=1, source_target_pairs={{0,2},{1,3},{2,0},{3,1},{4,6},{5,7},{6,4},{7,5},{8,10},{9,11},{10,... | collective-permute-start | bytes 1179656 | tf_op jit(solution)/shard_map/ppermute | solution.py:56
  53.6 6.0 %shard_map.95 = (bf16[128,3072]{1,0:T(8,128)(2,1)S(1)}, bf16[2,2,128,384]{3,2,1,0:T(8,128)(2,1)S(1)}, bf16[2,2,128,384]{3,2,1,0:T(8,128)(2,1)S(1)}, bf16[2,2,128...) custom-call(s32[10]{0:T(128)S(1)} %pad_add_fusion.info, s32[8,128]{1,0:T(8,128)S(1)} %bitcast.36, ...), custom_call_target="tpu_custom_call" | custom-call | flops 20132659200 | bytes 2359296 | tf_op jit(solution)/shard_map/pallas_call | solution.py:198
  60.3 2.4 %collective-permute-start.17 = (bf16[2,2,128,384]{3,2,1,0:T(8,128)(2,1)S(1)}, bf16[2,2,128,384]{3,2,1,0:T(8,128)(2,1)S(1)}, u32[]{:S(2)}, u32[]{:S(2)}) collective-permute-start(bf16[2,2,128,384]{3,2,1,0:T(8,128)(2,1)S(1)} %get-tuple-element.36), channel_id=1, source_target_pairs={{0,1},{1,2},{2,3},{3,0},{4,5},{5,6},{6,7},{7,4},{8,9},{9,10},{10,1... | collective-permute-start | bytes 1179656 | tf_op jit(solution)/shard_map/ppermute | solution.py:56
  62.7 9.2 %collective-permute-start.18 = (bf16[2,2,128,384]{3,2,1,0:T(8,128)(2,1)S(1)}, bf16[2,2,128,384]{3,2,1,0:T(8,128)(2,1)S(1)}, u32[]{:S(2)}, u32[]{:S(2)}) collective-permute-start(bf16[2,2,128,384]{3,2,1,0:T(8,128)(2,1)S(1)} %get-tuple-element.37), channel_id=1, source_target_pairs={{0,2},{1,3},{2,0},{3,1},{4,6},{5,7},{6,4},{7,5},{8,10},{9,11},{10,... | collective-permute-start | bytes 1179656 | tf_op jit(solution)/shard_map/ppermute | solution.py:56
  71.9 6.7 %collective-permute-start.11 = (bf16[128,3072]{1,0:T(8,128)(2,1)S(1)}, bf16[128,3072]{1,0:T(8,128)(2,1)S(1)}, u32[]{:S(2)}, u32[]{:S(2)}) collective-permute-start(bf16[128,3072]{1,0:T(8,128)(2,1)S(1)} %get-tuple-element.24), channel_id=1, source_target_pairs={{8,0},{16,8},{24,16},{32,24},{40,32},{48,40},{56,48},{64,56},{72,6... | collective-permute-start | bytes 2359304 | tf_op jit(solution)/shard_map/ppermute | solution.py:61
  78.6 4.2 %shard_map.96 = (bf16[128,2048]{1,0:T(8,128)(2,1)S(1)}, bf16[2,2,128,256]{3,2,1,0:T(8,128)(2,1)S(1)}, bf16[2,2,128,256]{3,2,1,0:T(8,128)(2,1)S(1)}, bf16[2,2,128...) custom-call(s32[10]{0:T(128)S(1)} %pad_add_fusion.info, s32[8,128]{1,0:T(8,128)S(1)} %bitcast.37, ...), custom_call_target="tpu_custom_call" | custom-call | flops 13421772800 | bytes 1572864 | tf_op jit(solution)/shard_map/pallas_call | solution.py:198
  82.9 2.4 %collective-permute-start.19 = (bf16[2,2,128,256]{3,2,1,0:T(8,128)(2,1)S(1)}, bf16[2,2,128,256]{3,2,1,0:T(8,128)(2,1)S(1)}, u32[]{:S(2)}, u32[]{:S(2)}) collective-permute-start(bf16[2,2,128,256]{3,2,1,0:T(8,128)(2,1)S(1)} %get-tuple-element.38), channel_id=1, source_target_pairs={{0,3},{1,0},{2,1},{3,2},{4,7},{5,4},{6,5},{7,6},{8,11},{9,8},{10,9... | collective-permute-start | bytes 786440 | tf_op jit(solution)/shard_map/ppermute | solution.py:56
  86.2 2.9 %collective-permute-start.21 = (bf16[2,2,128,256]{3,2,1,0:T(8,128)(2,1)S(1)}, bf16[2,2,128,256]{3,2,1,0:T(8,128)(2,1)S(1)}, u32[]{:S(2)}, u32[]{:S(2)}) collective-permute-start(bf16[2,2,128,256]{3,2,1,0:T(8,128)(2,1)S(1)} %get-tuple-element.40), channel_id=1, source_target_pairs={{0,2},{1,3},{2,0},{3,1},{4,6},{5,7},{6,4},{7,5},{8,10},{9,11},{10,... | collective-permute-start | bytes 786440 | tf_op jit(solution)/shard_map/ppermute | solution.py:56
  90.7 3.7 %collective-permute-done.19 = bf16[2,2,128,256]{3,2,1,0:T(8,128)(2,1)S(1)} collective-permute-done((bf16[2,2,128,256]{3,2,1,0:T(8,128)(2,1)S(1)}, bf16[2,2,128,256]{3,2,1,0:T(8,128)(2,1)S(1)}, u32[]{:S(2)}, u32[]{:S(2)}) %collective-permute-start.19) | collective-permute-done | bytes 262176 | tf_op jit(solution)/shard_map/ppermute | solution.py:56
  94.4 5.7 %collective-permute-start.15 = (bf16[128,2048]{1,0:T(8,128)(2,1)S(1)}, bf16[128,2048]{1,0:T(8,128)(2,1)S(1)}, u32[]{:S(2)}, u32[]{:S(2)}) collective-permute-start(bf16[128,2048]{1,0:T(8,128)(2,1)S(1)} %get-tuple-element.29), channel_id=1, source_target_pairs={{8,0},{16,8},{24,16},{32,24},{40,32},{48,40},{56,48},{64,56},{72,6... | collective-permute-start | bytes 1572872 | tf_op jit(solution)/shard_map/ppermute | solution.py:61
  101.6 6.5 %collective-permute-done.22 = bf16[2,128,768]{2,1,0:T(8,128)(2,1)S(1)} collective-permute-done((bf16[2,128,768]{2,1,0:T(8,128)(2,1)S(1)}, bf16[2,128,768]{2,1,0:T(8,128)(2,1)S(1)}, u32[]{:S(2)}, u32[]{:S(2)}) %collective-permute-start.22) | collective-permute-done | bytes 393248 | tf_op jit(solution)/shard_map/ppermute | solution.py:56
  109.6 14.0 %collective-permute-start.24 = (bf16[2,128,1024]{2,1,0:T(8,128)(2,1)S(1)}, bf16[2,128,1024]{2,1,0:T(8,128)(2,1)S(1)}, u32[]{:S(2)}, u32[]{:S(2)}) collective-permute-start(bf16[2,128,1024]{2,1,0:T(8,128)(2,1)S(1)} %add_convert_fusion), channel_id=1, source_target_pairs={{8,0},{16,8},{24,16},{32,24},{40,32},{48,40},{56,48},{64,56},{72,6... | collective-permute-start | bytes 1572872 | tf_op jit(solution)/shard_map/ppermute | solution.py:61
  123.6 1.5 %maximum_bitcast_fusion = bf16[1,128,8192]{2,1,0:T(8,128)(2,1)} fusion(bf16[128,2048]{1,0:T(8,128)(2,1)S(1)} %collective-permute-done.15, bf16[128,3072]{1,0:T(8,128)(2,1)S(1)} %collective-permute-done.11, bf16[128,3072]{1,0:T(8,128)(2,1)S(1)} %collective-permute-done.8), kind=kLoop, calls=%fused_computation | loop fusion | flops 6291456 | bytes 4194304 | tf_op jit(solution)/shard_map/broadcast_in_dim | solution.py:290
  125.1 5.2 %collective-permute-done.24 = bf16[2,128,1024]{2,1,0:T(8,128)(2,1)S(1)} collective-permute-done((bf16[2,128,1024]{2,1,0:T(8,128)(2,1)S(1)}, bf16[2,128,1024]{2,1,0:T(8,128)(2,1)S(1)}, u32[]{:S(2)}, u32[]{:S(2)}) %collective-permute-start.24) | collective-permute-done | bytes 524320 | tf_op jit(solution)/shard_map/ppermute | solution.py:61
  (62 shorter events, 15.9 us)
Async XLA Ops:
  2.5 9.6 %collective-permute-start.3 = (bf16[2,128,384]{2,1,0:T(8,128)(2,1)S(1)}, bf16[2,128,384]{2,1,0:T(8,128)(2,1)S(1)}, u32[]{:S(2)}, u32[]{:S(2)}) collective-permute-start(bf16[2,128,384]{2,1,0:T(8,128)(2,1)S(1)} %get-tuple-element.52.own_ref), channel_id=1, source_target_pairs={{0,1},{1,2},{2,3},{3,0},{4,5},{5,6},{6,7},{7,4},{8,9},{9,10},{10,1... | collective-permute-start | bytes 589832 | tf_op jit(solution)/shard_map/ppermute | solution.py:56
  4.1 9.4 %collective-permute-start.4 = (bf16[2,128,384]{2,1,0:T(8,128)(2,1)S(1)}, bf16[2,128,384]{2,1,0:T(8,128)(2,1)S(1)}, u32[]{:S(2)}, u32[]{:S(2)}) collective-permute-start(bf16[2,128,384]{2,1,0:T(8,128)(2,1)S(1)} %get-tuple-element.52.own_ref), channel_id=1, source_target_pairs={{0,3},{1,0},{2,1},{3,2},{4,7},{5,4},{6,5},{7,6},{8,11},{9,8},{10,9... | collective-permute-start | bytes 589832 | tf_op jit(solution)/shard_map/ppermute | solution.py:56
  5.0 10.3 %collective-permute-start.5 = (bf16[2,128,384]{2,1,0:T(8,128)(2,1)S(1)}, bf16[2,128,384]{2,1,0:T(8,128)(2,1)S(1)}, u32[]{:S(2)}, u32[]{:S(2)}) collective-permute-start(bf16[2,128,384]{2,1,0:T(8,128)(2,1)S(1)} %get-tuple-element.52.own_ref), channel_id=1, source_target_pairs={{0,4},{1,5},{2,6},{3,7},{8,12},{9,13},{10,14},{11,15},{16,20},{17,... | collective-permute-start | bytes 589832 | tf_op jit(solution)/shard_map/ppermute | solution.py:56
  10.1 9.4 %collective-permute-start = (bf16[2,128,640]{2,1,0:T(8,128)(2,1)S(1)}, bf16[2,128,640]{2,1,0:T(8,128)(2,1)S(1)}, u32[]{:S(2)}, u32[]{:S(2)}) collective-permute-start(bf16[2,128,640]{2,1,0:T(8,128)(2,1)S(1)} %get-tuple-element.48.own_ref), channel_id=1, source_target_pairs={{0,1},{1,2},{2,3},{3,0},{4,5},{5,6},{6,7},{7,4},{8,9},{9,10},{10,1... | collective-permute-start | bytes 983048 | tf_op jit(solution)/shard_map/ppermute | solution.py:56
  11.6 10.0 %collective-permute-start.1 = (bf16[2,128,640]{2,1,0:T(8,128)(2,1)S(1)}, bf16[2,128,640]{2,1,0:T(8,128)(2,1)S(1)}, u32[]{:S(2)}, u32[]{:S(2)}) collective-permute-start(bf16[2,128,640]{2,1,0:T(8,128)(2,1)S(1)} %get-tuple-element.48.own_ref), channel_id=1, source_target_pairs={{0,3},{1,0},{2,1},{3,2},{4,7},{5,4},{6,5},{7,6},{8,11},{9,8},{10,9... | collective-permute-start | bytes 983048 | tf_op jit(solution)/shard_map/ppermute | solution.py:56
  12.2 9.5 %collective-permute-start.2 = (bf16[2,128,640]{2,1,0:T(8,128)(2,1)S(1)}, bf16[2,128,640]{2,1,0:T(8,128)(2,1)S(1)}, u32[]{:S(2)}, u32[]{:S(2)}) collective-permute-start(bf16[2,128,640]{2,1,0:T(8,128)(2,1)S(1)} %get-tuple-element.48.own_ref), channel_id=1, source_target_pairs={{0,4},{1,5},{2,6},{3,7},{8,12},{9,13},{10,14},{11,15},{16,20},{17,... | collective-permute-start | bytes 983048 | tf_op jit(solution)/shard_map/ppermute | solution.py:56
  13.6 27.2 %collective-permute-start.7 = (bf16[2,2,128,384]{3,2,1,0:T(8,128)(2,1)S(1)}, bf16[2,2,128,384]{3,2,1,0:T(8,128)(2,1)S(1)}, u32[]{:S(2)}, u32[]{:S(2)}) collective-permute-start(bf16[2,2,128,384]{3,2,1,0:T(8,128)(2,1)S(1)} %pad_maximum_fusion.3), channel_id=1, source_target_pairs={{0,4},{1,5},{2,6},{3,7},{8,12},{9,13},{10,14},{11,15},{16,20},{17,... | collective-permute-start | bytes 1179656 | tf_op jit(solution)/shard_map/ppermute | solution.py:56
  15.3 25.5 %collective-permute-start.6 = (bf16[2,2,128,384]{3,2,1,0:T(8,128)(2,1)S(1)}, bf16[2,2,128,384]{3,2,1,0:T(8,128)(2,1)S(1)}, u32[]{:S(2)}, u32[]{:S(2)}) collective-permute-start(bf16[2,2,128,384]{3,2,1,0:T(8,128)(2,1)S(1)} %pad_maximum_fusion.2), channel_id=1, source_target_pairs={{0,2},{1,3},{2,0},{3,1},{4,6},{5,7},{6,4},{7,5},{8,10},{9,11},{10,... | collective-permute-start | bytes 1179656 | tf_op jit(solution)/shard_map/ppermute | solution.py:56
  21.7 28.4 %collective-permute-start.10 = (bf16[2,2,128,640]{3,2,1,0:T(8,128)(2,1)S(1)}, bf16[2,2,128,640]{3,2,1,0:T(8,128)(2,1)S(1)}, u32[]{:S(2)}, u32[]{:S(2)}) collective-permute-start(bf16[2,2,128,640]{3,2,1,0:T(8,128)(2,1)S(1)} %pad_maximum_fusion.1), channel_id=1, source_target_pairs={{0,4},{1,5},{2,6},{3,7},{8,12},{9,13},{10,14},{11,15},{16,20},{17,... | collective-permute-start | bytes 1966088 | tf_op jit(solution)/shard_map/ppermute | solution.py:56
  26.2 27.4 %collective-permute-start.9 = (bf16[2,2,128,640]{3,2,1,0:T(8,128)(2,1)S(1)}, bf16[2,2,128,640]{3,2,1,0:T(8,128)(2,1)S(1)}, u32[]{:S(2)}, u32[]{:S(2)}) collective-permute-start(bf16[2,2,128,640]{3,2,1,0:T(8,128)(2,1)S(1)} %pad_maximum_fusion), channel_id=1, source_target_pairs={{0,2},{1,3},{2,0},{3,1},{4,6},{5,7},{6,4},{7,5},{8,10},{9,11},{10,... | collective-permute-start | bytes 1966088 | tf_op jit(solution)/shard_map/ppermute | solution.py:56
  46.8 31.8 %collective-permute-start.8 = (bf16[128,3072]{1,0:T(8,128)(2,1)S(1)}, bf16[128,3072]{1,0:T(8,128)(2,1)S(1)}, u32[]{:S(2)}, u32[]{:S(2)}) collective-permute-start(bf16[128,3072]{1,0:T(8,128)(2,1)S(1)} %get-tuple-element.23), channel_id=1, source_target_pairs={{8,0},{16,8},{24,16},{32,24},{40,32},{48,40},{56,48},{64,56},{72,6... | collective-permute-start | bytes 2359304 | tf_op jit(solution)/shard_map/ppermute | solution.py:61
  46.9 13.5 %collective-permute-start.12 = (bf16[2,2,128,384]{3,2,1,0:T(8,128)(2,1)S(1)}, bf16[2,2,128,384]{3,2,1,0:T(8,128)(2,1)S(1)}, u32[]{:S(2)}, u32[]{:S(2)}) collective-permute-start(bf16[2,2,128,384]{3,2,1,0:T(8,128)(2,1)S(1)} %get-tuple-element.25), channel_id=1, source_target_pairs={{0,3},{1,0},{2,1},{3,2},{4,7},{5,4},{6,5},{7,6},{8,11},{9,8},{10,9... | collective-permute-start | bytes 1179656 | tf_op jit(solution)/shard_map/ppermute | solution.py:56
  47.0 15.7 %collective-permute-start.13 = (bf16[2,2,128,384]{3,2,1,0:T(8,128)(2,1)S(1)}, bf16[2,2,128,384]{3,2,1,0:T(8,128)(2,1)S(1)}, u32[]{:S(2)}, u32[]{:S(2)}) collective-permute-start(bf16[2,2,128,384]{3,2,1,0:T(8,128)(2,1)S(1)} %get-tuple-element.26), channel_id=1, source_target_pairs={{0,1},{1,2},{2,3},{3,0},{4,5},{5,6},{6,7},{7,4},{8,9},{9,10},{10,1... | collective-permute-start | bytes 1179656 | tf_op jit(solution)/shard_map/ppermute | solution.py:56
  50.1 21.8 %collective-permute-start.14 = (bf16[2,2,128,384]{3,2,1,0:T(8,128)(2,1)S(1)}, bf16[2,2,128,384]{3,2,1,0:T(8,128)(2,1)S(1)}, u32[]{:S(2)}, u32[]{:S(2)}) collective-permute-start(bf16[2,2,128,384]{3,2,1,0:T(8,128)(2,1)S(1)} %get-tuple-element.27), channel_id=1, source_target_pairs={{0,2},{1,3},{2,0},{3,1},{4,6},{5,7},{6,4},{7,5},{8,10},{9,11},{10,... | collective-permute-start | bytes 1179656 | tf_op jit(solution)/shard_map/ppermute | solution.py:56
  59.6 26.0 %collective-permute-start.16 = (bf16[2,2,128,384]{3,2,1,0:T(8,128)(2,1)S(1)}, bf16[2,2,128,384]{3,2,1,0:T(8,128)(2,1)S(1)}, u32[]{:S(2)}, u32[]{:S(2)}) collective-permute-start(bf16[2,2,128,384]{3,2,1,0:T(8,128)(2,1)S(1)} %get-tuple-element.35), channel_id=1, source_target_pairs={{0,3},{1,0},{2,1},{3,2},{4,7},{5,4},{6,5},{7,6},{8,11},{9,8},{10,9... | collective-permute-start | bytes 1179656 | tf_op jit(solution)/shard_map/ppermute | solution.py:56
  60.3 25.9 %collective-permute-start.17 = (bf16[2,2,128,384]{3,2,1,0:T(8,128)(2,1)S(1)}, bf16[2,2,128,384]{3,2,1,0:T(8,128)(2,1)S(1)}, u32[]{:S(2)}, u32[]{:S(2)}) collective-permute-start(bf16[2,2,128,384]{3,2,1,0:T(8,128)(2,1)S(1)} %get-tuple-element.36), channel_id=1, source_target_pairs={{0,1},{1,2},{2,3},{3,0},{4,5},{5,6},{6,7},{7,4},{8,9},{9,10},{10,1... | collective-permute-start | bytes 1179656 | tf_op jit(solution)/shard_map/ppermute | solution.py:56
  62.7 26.5 %collective-permute-start.18 = (bf16[2,2,128,384]{3,2,1,0:T(8,128)(2,1)S(1)}, bf16[2,2,128,384]{3,2,1,0:T(8,128)(2,1)S(1)}, u32[]{:S(2)}, u32[]{:S(2)}) collective-permute-start(bf16[2,2,128,384]{3,2,1,0:T(8,128)(2,1)S(1)} %get-tuple-element.37), channel_id=1, source_target_pairs={{0,2},{1,3},{2,0},{3,1},{4,6},{5,7},{6,4},{7,5},{8,10},{9,11},{10,... | collective-permute-start | bytes 1179656 | tf_op jit(solution)/shard_map/ppermute | solution.py:56
  71.9 51.7 %collective-permute-start.11 = (bf16[128,3072]{1,0:T(8,128)(2,1)S(1)}, bf16[128,3072]{1,0:T(8,128)(2,1)S(1)}, u32[]{:S(2)}, u32[]{:S(2)}) collective-permute-start(bf16[128,3072]{1,0:T(8,128)(2,1)S(1)} %get-tuple-element.24), channel_id=1, source_target_pairs={{8,0},{16,8},{24,16},{32,24},{40,32},{48,40},{56,48},{64,56},{72,6... | collective-permute-start | bytes 2359304 | tf_op jit(solution)/shard_map/ppermute | solution.py:61
  82.9 11.6 %collective-permute-start.19 = (bf16[2,2,128,256]{3,2,1,0:T(8,128)(2,1)S(1)}, bf16[2,2,128,256]{3,2,1,0:T(8,128)(2,1)S(1)}, u32[]{:S(2)}, u32[]{:S(2)}) collective-permute-start(bf16[2,2,128,256]{3,2,1,0:T(8,128)(2,1)S(1)} %get-tuple-element.38), channel_id=1, source_target_pairs={{0,3},{1,0},{2,1},{3,2},{4,7},{5,4},{6,5},{7,6},{8,11},{9,8},{10,9... | collective-permute-start | bytes 786440 | tf_op jit(solution)/shard_map/ppermute | solution.py:56
  85.6 14.6 %collective-permute-start.20 = (bf16[2,2,128,256]{3,2,1,0:T(8,128)(2,1)S(1)}, bf16[2,2,128,256]{3,2,1,0:T(8,128)(2,1)S(1)}, u32[]{:S(2)}, u32[]{:S(2)}) collective-permute-start(bf16[2,2,128,256]{3,2,1,0:T(8,128)(2,1)S(1)} %get-tuple-element.39), channel_id=1, source_target_pairs={{0,1},{1,2},{2,3},{3,0},{4,5},{5,6},{6,7},{7,4},{8,9},{9,10},{10,1... | collective-permute-start | bytes 786440 | tf_op jit(solution)/shard_map/ppermute | solution.py:56
  86.2 13.9 %collective-permute-start.21 = (bf16[2,2,128,256]{3,2,1,0:T(8,128)(2,1)S(1)}, bf16[2,2,128,256]{3,2,1,0:T(8,128)(2,1)S(1)}, u32[]{:S(2)}, u32[]{:S(2)}) collective-permute-start(bf16[2,2,128,256]{3,2,1,0:T(8,128)(2,1)S(1)} %get-tuple-element.40), channel_id=1, source_target_pairs={{0,2},{1,3},{2,0},{3,1},{4,6},{5,7},{6,4},{7,5},{8,10},{9,11},{10,... | collective-permute-start | bytes 786440 | tf_op jit(solution)/shard_map/ppermute | solution.py:56
  89.4 18.6 %collective-permute-start.22 = (bf16[2,128,768]{2,1,0:T(8,128)(2,1)S(1)}, bf16[2,128,768]{2,1,0:T(8,128)(2,1)S(1)}, u32[]{:S(2)}, u32[]{:S(2)}) collective-permute-start(bf16[2,128,768]{2,1,0:T(8,128)(2,1)S(1)} %pad_maximum_fusion.4), channel_id=1, source_target_pairs={{4,0},{5,1},{6,2},{7,3},{12,8},{13,9},{14,10},{15,11},{20,16},{21,... | collective-permute-start | bytes 1179656 | tf_op jit(solution)/shard_map/ppermute | solution.py:56
  94.4 29.2 %collective-permute-start.15 = (bf16[128,2048]{1,0:T(8,128)(2,1)S(1)}, bf16[128,2048]{1,0:T(8,128)(2,1)S(1)}, u32[]{:S(2)}, u32[]{:S(2)}) collective-permute-start(bf16[128,2048]{1,0:T(8,128)(2,1)S(1)} %get-tuple-element.29), channel_id=1, source_target_pairs={{8,0},{16,8},{24,16},{32,24},{40,32},{48,40},{56,48},{64,56},{72,6... | collective-permute-start | bytes 1572872 | tf_op jit(solution)/shard_map/ppermute | solution.py:61
  109.6 20.7 %collective-permute-start.24 = (bf16[2,128,1024]{2,1,0:T(8,128)(2,1)S(1)}, bf16[2,128,1024]{2,1,0:T(8,128)(2,1)S(1)}, u32[]{:S(2)}, u32[]{:S(2)}) collective-permute-start(bf16[2,128,1024]{2,1,0:T(8,128)(2,1)S(1)} %add_convert_fusion), channel_id=1, source_target_pairs={{8,0},{16,8},{24,16},{32,24},{40,32},{48,40},{56,48},{64,56},{72,6... | collective-permute-start | bytes 1572872 | tf_op jit(solution)/shard_map/ppermute | solution.py:61
  (6 other events, 124.9 us)

commit v3 on v2

--- a/solution.py
+++ b/solution.py
@@ -191,7 +191,7 @@
 def chunk_grads(by_block, at, base, groups, info, ends, queries, out_grad, own, from_left, from_right, from_y, from_x2, from_ylr):
     width = LANES
     wide = pl.BlockSpec((1, BLK, width), lambda g, *_: (0, 0, base + at + g))
-    one = pl.BlockSpec((2, BLK, HEAD_DIM), lambda g, *_: (0, 0, at + g))
+    one = pl.BlockSpec((2, BLK, HEAD_DIM), lambda g, *_: (0, 0, base + at + g))
     two = pl.BlockSpec((2, 2, BLK, HEAD_DIM), lambda g, *_: (0, 0, 0, at + g))
     outs = (NBLK,) if by_block else (2, 2, 2, 2)
     columns = groups * HEAD_DIM
@@ -262,15 +262,15 @@
             False, firsts[chunk] - base, base, SPLIT[chunk], held, ends, queries, out_grad, *gathered
         )
 
-    own0 = mine(0, 1)
-    near_round0 = near_round(own0)
-    far_round0 = far_round(own0, near_round0)
-    own12 = mine(1, 3)
-    near_round12 = near_round(own12)
-    far_round12 = far_round(own12, near_round12)
-    gathered12 = (own12, *near_round12, *far_round12)
-
-    dq0, stay0, *away0 = run(0, after(info, *near_round12), 0, own0, *near_round0, *far_round0)
+    own = mine(0, 3)
+    near = near_round(own)
+    cut = SPLIT[0] * HEAD_DIM
+    far_round0 = far_round(own[:, :, :cut], [part[:, :, :cut] for part in near])
+    rest = (own[:, :, cut:], [part[:, :, cut:] for part in near])
+    far_round12 = far_round(*rest)
+    gathered12 = (own, *near, *far_round12)
+
+    dq0, stay0, *away0 = run(0, info, 0, own, *near, *far_round0)
     moved0 = to_previous_section(dq0)
     back0 = reduce_x(*away0)
     dq1, stay1, *away1 = run(1, info, SPLIT[0], *gathered12)

time: 129 us -> 120 us (0.930); the launches traced: 131 us -> 119 us
  starting transfers between devices: 86 us -> 58.3 us
  waiting for transfers between devices: 19.6 us -> 36.2 us
    ppermute x21 -> x18, starting transfers between devices: 59.5 us -> 36.6 us  [send(): return lax.ppermute(block, 'ctx', ctx_route(move))]
    ppermute x21 -> x18, waiting for transfers between devices: 14.4 us -> 31 us  [send(): return lax.ppermute(block, 'ctx', ctx_route(move))]
    ppermute x4, starting transfers between devices: 26.5 us -> 21.7 us  [to_previous_section(): lax.ppermute(block, 'section', [((s + 1) % sections, s) for s in range(se...]
    slice x4 -> x0, local copies, waits for them, and re-layouts: 3.68 us -> none  [mine(): return jnp.concatenate([key_states[:, :, span], value_states[:, :, span]])]
  transfers between devices with their start and end apart: 25 -> 22, of which waited for: 6 -> 10; matrix products, arithmetic and copies ran while one was open for 4% -> 4% of each run, Pallas kernels for 12% -> 14%
where the time goes in v3:
time: 120 us; the launch traced here: 119 us
  starting transfers between devices  58.3 us (49%)
  waiting for transfers between devices  36.2 us (30%)
  Pallas kernels  16.3 us (14%)
  local copies, waits for them, and re-layouts  4.35 us (4%)
  other arithmetic  3.14 us (3%)
    ppermute x18, starting transfers between devices, send(): return lax.ppermute(block, 'ctx', ctx_route(move))  36.6 us
    ppermute x18, waiting for transfers between devices, send(): return lax.ppermute(block, 'ctx', ctx_route(move))  31 us
    ppermute x4, starting transfers between devices, to_previous_section(): lax.ppermute(block, 'section', [((s + 1) % sections, s) for s in range(se...  21.7 us
    pallas_call x3, Pallas kernels, chunk_grads(): pl.pallas_call(functools.partial(grads_kernel, by_block), grid_spec=pltpu...  16.3 us
    ppermute x4, waiting for transfers between devices, to_previous_section(): lax.ppermute(block, 'section', [((s + 1) % sections, s) for s in range(se...  5.24 us
  transfers between devices with their start and end apart: 22, of which 10 were waited for; matrix products, arithmetic and copies ran while one was open for 4% of the time, Pallas kernels for 14%

profile of v3, /device:TPU:2, one launch (start us, length us, event | category | flops | bytes accessed | tf_op | source)
XLA Modules:
  0.0 119.3 jit_solution(14507292434905971465)
XLA Ops:
  2.6 2.3 %collective-permute-start.1 = (bf16[2,128,1024]{2,1,0:T(8,128)(2,1)S(1)}, bf16[2,128,1024]{2,1,0:T(8,128)(2,1)S(1)}, u32[]{:S(2)}, u32[]{:S(2)}) collective-permute-start(bf16[2,128,1024]{2,1,0:T(8,128)(2,1)S(1)} %constant_dynamic-update-slice_fusion.own_ref), channel_id=1, source_target_pairs={{0,3},{1,0},{2,1},{3,2},{4,7},{5,4},{6,5},{7,6},{8,11},{9,8},{10,9... | collective-permute-start | bytes 1572872 | tf_op jit(solution)/shard_map/ppermute | solution.py:56
  4.9 3.3 %collective-permute-start.2 = (bf16[2,128,1024]{2,1,0:T(8,128)(2,1)S(1)}, bf16[2,128,1024]{2,1,0:T(8,128)(2,1)S(1)}, u32[]{:S(2)}, u32[]{:S(2)}) collective-permute-start(bf16[2,128,1024]{2,1,0:T(8,128)(2,1)S(1)} %constant_dynamic-update-slice_fusion.own_ref), channel_id=1, source_target_pairs={{0,4},{1,5},{2,6},{3,7},{8,12},{9,13},{10,14},{11,15},{16,20},{17,... | collective-permute-start | bytes 1572872 | tf_op jit(solution)/shard_map/ppermute | solution.py:56
  10.2 6.1 %collective-permute-done.1.right_ref = bf16[2,128,1024]{2,1,0:T(8,128)(2,1)S(1)} collective-permute-done((bf16[2,128,1024]{2,1,0:T(8,128)(2,1)S(1)}, bf16[2,128,1024]{2,1,0:T(8,128)(2,1)S(1)}, u32[]{:S(2)}, u32[]{:S(2)}) %collective-permute-start.1) | collective-permute-done | bytes 524320 | tf_op jit(solution)/shard_map/ppermute | solution.py:56
  17.7 3.5 %collective-permute-start.4 = (bf16[2,2,128,384]{3,2,1,0:T(8,128)(2,1)S(1)}, bf16[2,2,128,384]{3,2,1,0:T(8,128)(2,1)S(1)}, u32[]{:S(2)}, u32[]{:S(2)}) collective-permute-start(bf16[2,2,128,384]{3,2,1,0:T(8,128)(2,1)S(1)} %pad_maximum_fusion.3), channel_id=1, source_target_pairs={{0,4},{1,5},{2,6},{3,7},{8,12},{9,13},{10,14},{11,15},{16,20},{17,... | collective-permute-start | bytes 1179656 | tf_op jit(solution)/shard_map/ppermute | solution.py:56
  21.3 2.2 %collective-permute-start.3 = (bf16[2,2,128,384]{3,2,1,0:T(8,128)(2,1)S(1)}, bf16[2,2,128,384]{3,2,1,0:T(8,128)(2,1)S(1)}, u32[]{:S(2)}, u32[]{:S(2)}) collective-permute-start(bf16[2,2,128,384]{3,2,1,0:T(8,128)(2,1)S(1)} %pad_maximum_fusion.2), channel_id=1, source_target_pairs={{0,2},{1,3},{2,0},{3,1},{4,6},{5,7},{6,4},{7,5},{8,10},{9,11},{10,... | collective-permute-start | bytes 1179656 | tf_op jit(solution)/shard_map/ppermute | solution.py:56
  23.7 3.5 %collective-permute-start.7 = (bf16[2,2,128,640]{3,2,1,0:T(8,128)(2,1)S(1)}, bf16[2,2,128,640]{3,2,1,0:T(8,128)(2,1)S(1)}, u32[]{:S(2)}, u32[]{:S(2)}) collective-permute-start(bf16[2,2,128,640]{3,2,1,0:T(8,128)(2,1)S(1)} %pad_maximum_fusion.1), channel_id=1, source_target_pairs={{0,4},{1,5},{2,6},{3,7},{8,12},{9,13},{10,14},{11,15},{16,20},{17,... | collective-permute-start | bytes 1966088 | tf_op jit(solution)/shard_map/ppermute | solution.py:56
  27.6 3.2 %collective-permute-done.4.ylr_ref = bf16[2,2,128,384]{3,2,1,0:T(8,128)(2,1)S(1)} collective-permute-done((bf16[2,2,128,384]{3,2,1,0:T(8,128)(2,1)S(1)}, bf16[2,2,128,384]{3,2,1,0:T(8,128)(2,1)S(1)}, u32[]{:S(2)}, u32[]{:S(2)}) %collective-permute-start.4) | collective-permute-done | bytes 393248 | tf_op jit(solution)/shard_map/ppermute | solution.py:56
  30.7 4.2 %collective-permute-done.3.x2_ref = bf16[2,2,128,384]{3,2,1,0:T(8,128)(2,1)S(1)} collective-permute-done((bf16[2,2,128,384]{3,2,1,0:T(8,128)(2,1)S(1)}, bf16[2,2,128,384]{3,2,1,0:T(8,128)(2,1)S(1)}, u32[]{:S(2)}, u32[]{:S(2)}) %collective-permute-start.3) | collective-permute-done | bytes 393248 | tf_op jit(solution)/shard_map/ppermute | solution.py:56
  34.9 6.0 %shard_map.94 = (bf16[128,3072]{1,0:T(8,128)(2,1)S(1)}, bf16[2,2,128,384]{3,2,1,0:T(8,128)(2,1)S(1)}, bf16[2,2,128,384]{3,2,1,0:T(8,128)(2,1)S(1)}, bf16[2,2,128...) custom-call(s32[10]{0:T(128)S(1)} %pad_add_fusion.info, s32[8,128]{1,0:T(8,128)S(1)} %bitcast.35, ...), custom_call_target="tpu_custom_call" | custom-call | flops 20132659200 | bytes 2359296 | tf_op jit(solution)/shard_map/pallas_call | solution.py:198
  41.0 3.3 %collective-permute-start.5 = (bf16[128,3072]{1,0:T(8,128)(2,1)S(1)}, bf16[128,3072]{1,0:T(8,128)(2,1)S(1)}, u32[]{:S(2)}, u32[]{:S(2)}) collective-permute-start(bf16[128,3072]{1,0:T(8,128)(2,1)S(1)} %get-tuple-element.21), channel_id=1, source_target_pairs={{8,0},{16,8},{24,16},{32,24},{40,32},{48,40},{56,48},{64,56},{72,6... | collective-permute-start | bytes 2359304 | tf_op jit(solution)/shard_map/ppermute | solution.py:61
  44.2 4.2 %collective-permute-start.10 = (bf16[2,2,128,384]{3,2,1,0:T(8,128)(2,1)S(1)}, bf16[2,2,128,384]{3,2,1,0:T(8,128)(2,1)S(1)}, u32[]{:S(2)}, u32[]{:S(2)}) collective-permute-start(bf16[2,2,128,384]{3,2,1,0:T(8,128)(2,1)S(1)} %get-tuple-element.24), channel_id=1, source_target_pairs={{0,1},{1,2},{2,3},{3,0},{4,5},{5,6},{6,7},{7,4},{8,9},{9,10},{10,1... | collective-permute-start | bytes 1179656 | tf_op jit(solution)/shard_map/ppermute | solution.py:56
  49.7 2.6 %collective-permute-start.9 = (bf16[2,2,128,384]{3,2,1,0:T(8,128)(2,1)S(1)}, bf16[2,2,128,384]{3,2,1,0:T(8,128)(2,1)S(1)}, u32[]{:S(2)}, u32[]{:S(2)}) collective-permute-start(bf16[2,2,128,384]{3,2,1,0:T(8,128)(2,1)S(1)} %get-tuple-element.23), channel_id=1, source_target_pairs={{0,3},{1,0},{2,1},{3,2},{4,7},{5,4},{6,5},{7,6},{8,11},{9,8},{10,9... | collective-permute-start | bytes 1179656 | tf_op jit(solution)/shard_map/ppermute | solution.py:56
  52.3 6.0 %shard_map.95 = (bf16[128,3072]{1,0:T(8,128)(2,1)S(1)}, bf16[2,2,128,384]{3,2,1,0:T(8,128)(2,1)S(1)}, bf16[2,2,128,384]{3,2,1,0:T(8,128)(2,1)S(1)}, bf16[2,2,128...) custom-call(s32[10]{0:T(128)S(1)} %pad_add_fusion.info, s32[8,128]{1,0:T(8,128)S(1)} %bitcast.36, ...), custom_call_target="tpu_custom_call" | custom-call | flops 20132659200 | bytes 2359296 | tf_op jit(solution)/shard_map/pallas_call | solution.py:198
  59.2 3.3 %collective-permute-done.10 = bf16[2,2,128,384]{3,2,1,0:T(8,128)(2,1)S(1)} collective-permute-done((bf16[2,2,128,384]{3,2,1,0:T(8,128)(2,1)S(1)}, bf16[2,2,128,384]{3,2,1,0:T(8,128)(2,1)S(1)}, u32[]{:S(2)}, u32[]{:S(2)}) %collective-permute-start.10) | collective-permute-done | bytes 393248 | tf_op jit(solution)/shard_map/ppermute | solution.py:56
  62.5 3.0 %collective-permute-start.14 = (bf16[2,2,128,384]{3,2,1,0:T(8,128)(2,1)S(1)}, bf16[2,2,128,384]{3,2,1,0:T(8,128)(2,1)S(1)}, u32[]{:S(2)}, u32[]{:S(2)}) collective-permute-start(bf16[2,2,128,384]{3,2,1,0:T(8,128)(2,1)S(1)} %get-tuple-element.34), channel_id=1, source_target_pairs={{0,1},{1,2},{2,3},{3,0},{4,5},{5,6},{6,7},{7,4},{8,9},{9,10},{10,1... | collective-permute-start | bytes 1179656 | tf_op jit(solution)/shard_map/ppermute | solution.py:56
  67.7 6.6 %collective-permute-start.8 = (bf16[128,3072]{1,0:T(8,128)(2,1)S(1)}, bf16[128,3072]{1,0:T(8,128)(2,1)S(1)}, u32[]{:S(2)}, u32[]{:S(2)}) collective-permute-start(bf16[128,3072]{1,0:T(8,128)(2,1)S(1)} %get-tuple-element.22), channel_id=1, source_target_pairs={{8,0},{16,8},{24,16},{32,24},{40,32},{48,40},{56,48},{64,56},{72,6... | collective-permute-start | bytes 2359304 | tf_op jit(solution)/shard_map/ppermute | solution.py:61
  74.3 4.3 %shard_map.96 = (bf16[128,2048]{1,0:T(8,128)(2,1)S(1)}, bf16[2,2,128,256]{3,2,1,0:T(8,128)(2,1)S(1)}, bf16[2,2,128,256]{3,2,1,0:T(8,128)(2,1)S(1)}, bf16[2,2,128...) custom-call(s32[10]{0:T(128)S(1)} %pad_add_fusion.info, s32[8,128]{1,0:T(8,128)S(1)} %bitcast.37, ...), custom_call_target="tpu_custom_call" | custom-call | flops 13421772800 | bytes 1572864 | tf_op jit(solution)/shard_map/pallas_call | solution.py:198
  79.1 2.6 %collective-permute-start.17 = (bf16[2,2,128,256]{3,2,1,0:T(8,128)(2,1)S(1)}, bf16[2,2,128,256]{3,2,1,0:T(8,128)(2,1)S(1)}, u32[]{:S(2)}, u32[]{:S(2)}) collective-permute-start(bf16[2,2,128,256]{3,2,1,0:T(8,128)(2,1)S(1)} %get-tuple-element.37), channel_id=1, source_target_pairs={{0,1},{1,2},{2,3},{3,0},{4,5},{5,6},{6,7},{7,4},{8,9},{9,10},{10,1... | collective-permute-start | bytes 786440 | tf_op jit(solution)/shard_map/ppermute | solution.py:56
  81.8 4.1 %collective-permute-start.18 = (bf16[2,2,128,256]{3,2,1,0:T(8,128)(2,1)S(1)}, bf16[2,2,128,256]{3,2,1,0:T(8,128)(2,1)S(1)}, u32[]{:S(2)}, u32[]{:S(2)}) collective-permute-start(bf16[2,2,128,256]{3,2,1,0:T(8,128)(2,1)S(1)} %get-tuple-element.38), channel_id=1, source_target_pairs={{0,2},{1,3},{2,0},{3,1},{4,6},{5,7},{6,4},{7,5},{8,10},{9,11},{10,... | collective-permute-start | bytes 786440 | tf_op jit(solution)/shard_map/ppermute | solution.py:56
  87.5 3.4 %collective-permute-done.16 = bf16[2,2,128,256]{3,2,1,0:T(8,128)(2,1)S(1)} collective-permute-done((bf16[2,2,128,256]{3,2,1,0:T(8,128)(2,1)S(1)}, bf16[2,2,128,256]{3,2,1,0:T(8,128)(2,1)S(1)}, u32[]{:S(2)}, u32[]{:S(2)}) %collective-permute-start.16) | collective-permute-done | bytes 262176 | tf_op jit(solution)/shard_map/ppermute | solution.py:56
  90.9 6.7 %collective-permute-start.12 = (bf16[128,2048]{1,0:T(8,128)(2,1)S(1)}, bf16[128,2048]{1,0:T(8,128)(2,1)S(1)}, u32[]{:S(2)}, u32[]{:S(2)}) collective-permute-start(bf16[128,2048]{1,0:T(8,128)(2,1)S(1)} %get-tuple-element.27), channel_id=1, source_target_pairs={{8,0},{16,8},{24,16},{32,24},{40,32},{48,40},{56,48},{64,56},{72,6... | collective-permute-start | bytes 1572872 | tf_op jit(solution)/shard_map/ppermute | solution.py:61
  100.2 6.2 %collective-permute-done.20 = bf16[2,128,256]{2,1,0:T(8,128)(2,1)S(1)} collective-permute-done((bf16[2,128,256]{2,1,0:T(8,128)(2,1)S(1)}, bf16[2,128,256]{2,1,0:T(8,128)(2,1)S(1)}, u32[]{:S(2)}, u32[]{:S(2)}) %collective-permute-start.20) | collective-permute-done | bytes 131104 | tf_op jit(solution)/shard_map/ppermute | solution.py:56
  106.6 5.2 %collective-permute-start.21 = (bf16[2,128,1024]{2,1,0:T(8,128)(2,1)S(1)}, bf16[2,128,1024]{2,1,0:T(8,128)(2,1)S(1)}, u32[]{:S(2)}, u32[]{:S(2)}) collective-permute-start(bf16[2,128,1024]{2,1,0:T(8,128)(2,1)S(1)} %add_convert_fusion), channel_id=1, source_target_pairs={{8,0},{16,8},{24,16},{32,24},{40,32},{48,40},{56,48},{64,56},{72,6... | collective-permute-start | bytes 1572872 | tf_op jit(solution)/shard_map/ppermute | solution.py:61
  113.2 5.2 %collective-permute-done.21 = bf16[2,128,1024]{2,1,0:T(8,128)(2,1)S(1)} collective-permute-done((bf16[2,128,1024]{2,1,0:T(8,128)(2,1)S(1)}, bf16[2,128,1024]{2,1,0:T(8,128)(2,1)S(1)}, u32[]{:S(2)}, u32[]{:S(2)}) %collective-permute-start.21) | collective-permute-done | bytes 524320 | tf_op jit(solution)/shard_map/ppermute | solution.py:61
  (58 shorter events, 17.4 us)
Async XLA Ops:
  2.6 13.7 %collective-permute-start.1 = (bf16[2,128,1024]{2,1,0:T(8,128)(2,1)S(1)}, bf16[2,128,1024]{2,1,0:T(8,128)(2,1)S(1)}, u32[]{:S(2)}, u32[]{:S(2)}) collective-permute-start(bf16[2,128,1024]{2,1,0:T(8,128)(2,1)S(1)} %constant_dynamic-update-slice_fusion.own_ref), channel_id=1, source_target_pairs={{0,3},{1,0},{2,1},{3,2},{4,7},{5,4},{6,5},{7,6},{8,11},{9,8},{10,9... | collective-permute-start | bytes 1572872 | tf_op jit(solution)/shard_map/ppermute | solution.py:56
  4.9 12.7 %collective-permute-start = (bf16[2,128,1024]{2,1,0:T(8,128)(2,1)S(1)}, bf16[2,128,1024]{2,1,0:T(8,128)(2,1)S(1)}, u32[]{:S(2)}, u32[]{:S(2)}) collective-permute-start(bf16[2,128,1024]{2,1,0:T(8,128)(2,1)S(1)} %constant_dynamic-update-slice_fusion.own_ref), channel_id=1, source_target_pairs={{0,1},{1,2},{2,3},{3,0},{4,5},{5,6},{6,7},{7,4},{8,9},{9,10},{10,1... | collective-permute-start | bytes 1572872 | tf_op jit(solution)/shard_map/ppermute | solution.py:56
  4.9 16.3 %collective-permute-start.2 = (bf16[2,128,1024]{2,1,0:T(8,128)(2,1)S(1)}, bf16[2,128,1024]{2,1,0:T(8,128)(2,1)S(1)}, u32[]{:S(2)}, u32[]{:S(2)}) collective-permute-start(bf16[2,128,1024]{2,1,0:T(8,128)(2,1)S(1)} %constant_dynamic-update-slice_fusion.own_ref), channel_id=1, source_target_pairs={{0,4},{1,5},{2,6},{3,7},{8,12},{9,13},{10,14},{11,15},{16,20},{17,... | collective-permute-start | bytes 1572872 | tf_op jit(solution)/shard_map/ppermute | solution.py:56
  17.7 13.0 %collective-permute-start.4 = (bf16[2,2,128,384]{3,2,1,0:T(8,128)(2,1)S(1)}, bf16[2,2,128,384]{3,2,1,0:T(8,128)(2,1)S(1)}, u32[]{:S(2)}, u32[]{:S(2)}) collective-permute-start(bf16[2,2,128,384]{3,2,1,0:T(8,128)(2,1)S(1)} %pad_maximum_fusion.3), channel_id=1, source_target_pairs={{0,4},{1,5},{2,6},{3,7},{8,12},{9,13},{10,14},{11,15},{16,20},{17,... | collective-permute-start | bytes 1179656 | tf_op jit(solution)/shard_map/ppermute | solution.py:56
  21.3 13.6 %collective-permute-start.3 = (bf16[2,2,128,384]{3,2,1,0:T(8,128)(2,1)S(1)}, bf16[2,2,128,384]{3,2,1,0:T(8,128)(2,1)S(1)}, u32[]{:S(2)}, u32[]{:S(2)}) collective-permute-start(bf16[2,2,128,384]{3,2,1,0:T(8,128)(2,1)S(1)} %pad_maximum_fusion.2), channel_id=1, source_target_pairs={{0,2},{1,3},{2,0},{3,1},{4,6},{5,7},{6,4},{7,5},{8,10},{9,11},{10,... | collective-permute-start | bytes 1179656 | tf_op jit(solution)/shard_map/ppermute | solution.py:56
  23.5 11.5 %copy-start.2 = (bf16[1,128,8192]{2,1,0:T(8,128)(2,1)S(1)}, bf16[1,128,8192]{2,1,0:T(8,128)(2,1)}, u32[]{:S(2)}) copy-start(bf16[1,128,8192]{2,1,0:T(8,128)(2,1)} %g_ref.5) | copy-start | bytes 6291460
  23.5 11.4 %copy-start.1 = (bf16[1,128,8192]{2,1,0:T(8,128)(2,1)S(1)}, bf16[1,128,8192]{2,1,0:T(8,128)(2,1)}, u32[]{:S(2)}) copy-start(bf16[1,128,8192]{2,1,0:T(8,128)(2,1)} %q_ref.5) | copy-start | bytes 6291460
  23.7 26.0 %collective-permute-start.7 = (bf16[2,2,128,640]{3,2,1,0:T(8,128)(2,1)S(1)}, bf16[2,2,128,640]{3,2,1,0:T(8,128)(2,1)S(1)}, u32[]{:S(2)}, u32[]{:S(2)}) collective-permute-start(bf16[2,2,128,640]{3,2,1,0:T(8,128)(2,1)S(1)} %pad_maximum_fusion.1), channel_id=1, source_target_pairs={{0,4},{1,5},{2,6},{3,7},{8,12},{9,13},{10,14},{11,15},{16,20},{17,... | collective-permute-start | bytes 1966088 | tf_op jit(solution)/shard_map/ppermute | solution.py:56
  27.3 25.0 %collective-permute-start.6 = (bf16[2,2,128,640]{3,2,1,0:T(8,128)(2,1)S(1)}, bf16[2,2,128,640]{3,2,1,0:T(8,128)(2,1)S(1)}, u32[]{:S(2)}, u32[]{:S(2)}) collective-permute-start(bf16[2,2,128,640]{3,2,1,0:T(8,128)(2,1)S(1)} %pad_maximum_fusion), channel_id=1, source_target_pairs={{0,2},{1,3},{2,0},{3,1},{4,6},{5,7},{6,4},{7,5},{8,10},{9,11},{10,... | collective-permute-start | bytes 1966088 | tf_op jit(solution)/shard_map/ppermute | solution.py:56
  41.0 33.3 %collective-permute-start.5 = (bf16[128,3072]{1,0:T(8,128)(2,1)S(1)}, bf16[128,3072]{1,0:T(8,128)(2,1)S(1)}, u32[]{:S(2)}, u32[]{:S(2)}) collective-permute-start(bf16[128,3072]{1,0:T(8,128)(2,1)S(1)} %get-tuple-element.21), channel_id=1, source_target_pairs={{8,0},{16,8},{24,16},{32,24},{40,32},{48,40},{56,48},{64,56},{72,6... | collective-permute-start | bytes 2359304 | tf_op jit(solution)/shard_map/ppermute | solution.py:61
  44.2 18.3 %collective-permute-start.10 = (bf16[2,2,128,384]{3,2,1,0:T(8,128)(2,1)S(1)}, bf16[2,2,128,384]{3,2,1,0:T(8,128)(2,1)S(1)}, u32[]{:S(2)}, u32[]{:S(2)}) collective-permute-start(bf16[2,2,128,384]{3,2,1,0:T(8,128)(2,1)S(1)} %get-tuple-element.24), channel_id=1, source_target_pairs={{0,1},{1,2},{2,3},{3,0},{4,5},{5,6},{6,7},{7,4},{8,9},{9,10},{10,1... | collective-permute-start | bytes 1179656 | tf_op jit(solution)/shard_map/ppermute | solution.py:56
  48.4 17.1 %collective-permute-start.11 = (bf16[2,2,128,384]{3,2,1,0:T(8,128)(2,1)S(1)}, bf16[2,2,128,384]{3,2,1,0:T(8,128)(2,1)S(1)}, u32[]{:S(2)}, u32[]{:S(2)}) collective-permute-start(bf16[2,2,128,384]{3,2,1,0:T(8,128)(2,1)S(1)} %get-tuple-element.25), channel_id=1, source_target_pairs={{0,2},{1,3},{2,0},{3,1},{4,6},{5,7},{6,4},{7,5},{8,10},{9,11},{10,... | collective-permute-start | bytes 1179656 | tf_op jit(solution)/shard_map/ppermute | solution.py:56
  49.7 18.0 %collective-permute-start.9 = (bf16[2,2,128,384]{3,2,1,0:T(8,128)(2,1)S(1)}, bf16[2,2,128,384]{3,2,1,0:T(8,128)(2,1)S(1)}, u32[]{:S(2)}, u32[]{:S(2)}) collective-permute-start(bf16[2,2,128,384]{3,2,1,0:T(8,128)(2,1)S(1)} %get-tuple-element.23), channel_id=1, source_target_pairs={{0,3},{1,0},{2,1},{3,2},{4,7},{5,4},{6,5},{7,6},{8,11},{9,8},{10,9... | collective-permute-start | bytes 1179656 | tf_op jit(solution)/shard_map/ppermute | solution.py:56
  58.4 20.8 %collective-permute-start.13 = (bf16[2,2,128,384]{3,2,1,0:T(8,128)(2,1)S(1)}, bf16[2,2,128,384]{3,2,1,0:T(8,128)(2,1)S(1)}, u32[]{:S(2)}, u32[]{:S(2)}) collective-permute-start(bf16[2,2,128,384]{3,2,1,0:T(8,128)(2,1)S(1)} %get-tuple-element.33), channel_id=1, source_target_pairs={{0,3},{1,0},{2,1},{3,2},{4,7},{5,4},{6,5},{7,6},{8,11},{9,8},{10,9... | collective-permute-start | bytes 1179656 | tf_op jit(solution)/shard_map/ppermute | solution.py:56
  62.5 19.2 %collective-permute-start.14 = (bf16[2,2,128,384]{3,2,1,0:T(8,128)(2,1)S(1)}, bf16[2,2,128,384]{3,2,1,0:T(8,128)(2,1)S(1)}, u32[]{:S(2)}, u32[]{:S(2)}) collective-permute-start(bf16[2,2,128,384]{3,2,1,0:T(8,128)(2,1)S(1)} %get-tuple-element.34), channel_id=1, source_target_pairs={{0,1},{1,2},{2,3},{3,0},{4,5},{5,6},{6,7},{7,4},{8,9},{9,10},{10,1... | collective-permute-start | bytes 1179656 | tf_op jit(solution)/shard_map/ppermute | solution.py:56
  65.5 20.4 %collective-permute-start.15 = (bf16[2,2,128,384]{3,2,1,0:T(8,128)(2,1)S(1)}, bf16[2,2,128,384]{3,2,1,0:T(8,128)(2,1)S(1)}, u32[]{:S(2)}, u32[]{:S(2)}) collective-permute-start(bf16[2,2,128,384]{3,2,1,0:T(8,128)(2,1)S(1)} %get-tuple-element.35), channel_id=1, source_target_pairs={{0,2},{1,3},{2,0},{3,1},{4,6},{5,7},{6,4},{7,5},{8,10},{9,11},{10,... | collective-permute-start | bytes 1179656 | tf_op jit(solution)/shard_map/ppermute | solution.py:56
  67.7 44.0 %collective-permute-start.8 = (bf16[128,3072]{1,0:T(8,128)(2,1)S(1)}, bf16[128,3072]{1,0:T(8,128)(2,1)S(1)}, u32[]{:S(2)}, u32[]{:S(2)}) collective-permute-start(bf16[128,3072]{1,0:T(8,128)(2,1)S(1)} %get-tuple-element.22), channel_id=1, source_target_pairs={{8,0},{16,8},{24,16},{32,24},{40,32},{48,40},{56,48},{64,56},{72,6... | collective-permute-start | bytes 2359304 | tf_op jit(solution)/shard_map/ppermute | solution.py:61
  78.6 12.3 %collective-permute-start.16 = (bf16[2,2,128,256]{3,2,1,0:T(8,128)(2,1)S(1)}, bf16[2,2,128,256]{3,2,1,0:T(8,128)(2,1)S(1)}, u32[]{:S(2)}, u32[]{:S(2)}) collective-permute-start(bf16[2,2,128,256]{3,2,1,0:T(8,128)(2,1)S(1)} %get-tuple-element.36), channel_id=1, source_target_pairs={{0,3},{1,0},{2,1},{3,2},{4,7},{5,4},{6,5},{7,6},{8,11},{9,8},{10,9... | collective-permute-start | bytes 786440 | tf_op jit(solution)/shard_map/ppermute | solution.py:56
  79.1 18.5 %collective-permute-start.17 = (bf16[2,2,128,256]{3,2,1,0:T(8,128)(2,1)S(1)}, bf16[2,2,128,256]{3,2,1,0:T(8,128)(2,1)S(1)}, u32[]{:S(2)}, u32[]{:S(2)}) collective-permute-start(bf16[2,2,128,256]{3,2,1,0:T(8,128)(2,1)S(1)} %get-tuple-element.37), channel_id=1, source_target_pairs={{0,1},{1,2},{2,3},{3,0},{4,5},{5,6},{6,7},{7,4},{8,9},{9,10},{10,1... | collective-permute-start | bytes 786440 | tf_op jit(solution)/shard_map/ppermute | solution.py:56
  81.8 15.9 %collective-permute-start.18 = (bf16[2,2,128,256]{3,2,1,0:T(8,128)(2,1)S(1)}, bf16[2,2,128,256]{3,2,1,0:T(8,128)(2,1)S(1)}, u32[]{:S(2)}, u32[]{:S(2)}) collective-permute-start(bf16[2,2,128,256]{3,2,1,0:T(8,128)(2,1)S(1)} %get-tuple-element.38), channel_id=1, source_target_pairs={{0,2},{1,3},{2,0},{3,1},{4,6},{5,7},{6,4},{7,5},{8,10},{9,11},{10,... | collective-permute-start | bytes 786440 | tf_op jit(solution)/shard_map/ppermute | solution.py:56
  86.2 14.0 %collective-permute-start.19 = (bf16[2,128,768]{2,1,0:T(8,128)(2,1)S(1)}, bf16[2,128,768]{2,1,0:T(8,128)(2,1)S(1)}, u32[]{:S(2)}, u32[]{:S(2)}) collective-permute-start(bf16[2,128,768]{2,1,0:T(8,128)(2,1)S(1)} %pad_maximum_fusion.4), channel_id=1, source_target_pairs={{4,0},{5,1},{6,2},{7,3},{12,8},{13,9},{14,10},{15,11},{20,16},{21,... | collective-permute-start | bytes 1179656 | tf_op jit(solution)/shard_map/ppermute | solution.py:56
  90.9 20.8 %collective-permute-start.12 = (bf16[128,2048]{1,0:T(8,128)(2,1)S(1)}, bf16[128,2048]{1,0:T(8,128)(2,1)S(1)}, u32[]{:S(2)}, u32[]{:S(2)}) collective-permute-start(bf16[128,2048]{1,0:T(8,128)(2,1)S(1)} %get-tuple-element.27), channel_id=1, source_target_pairs={{8,0},{16,8},{24,16},{32,24},{40,32},{48,40},{56,48},{64,56},{72,6... | collective-permute-start | bytes 1572872 | tf_op jit(solution)/shard_map/ppermute | solution.py:61
  97.8 8.6 %collective-permute-start.20 = (bf16[2,128,256]{2,1,0:T(8,128)(2,1)S(1)}, bf16[2,128,256]{2,1,0:T(8,128)(2,1)S(1)}, u32[]{:S(2)}, u32[]{:S(2)}) collective-permute-start(bf16[2,128,256]{2,1,0:T(8,128)(2,1)S(1)} %get-tuple-element.45), channel_id=1, source_target_pairs={{4,0},{5,1},{6,2},{7,3},{12,8},{13,9},{14,10},{15,11},{20,16},{21,... | collective-permute-start | bytes 393224 | tf_op jit(solution)/shard_map/ppermute | solution.py:56
  106.6 11.9 %collective-permute-start.21 = (bf16[2,128,1024]{2,1,0:T(8,128)(2,1)S(1)}, bf16[2,128,1024]{2,1,0:T(8,128)(2,1)S(1)}, u32[]{:S(2)}, u32[]{:S(2)}) collective-permute-start(bf16[2,128,1024]{2,1,0:T(8,128)(2,1)S(1)} %add_convert_fusion), channel_id=1, source_target_pairs={{8,0},{16,8},{24,16},{32,24},{40,32},{48,40},{56,48},{64,56},{72,6... | collective-permute-start | bytes 1572872 | tf_op jit(solution)/shard_map/ppermute | solution.py:61
  (2 other events, 20.3 us)

commit v4 on v3

--- a/solution.py
+++ b/solution.py
@@ -161,13 +161,13 @@
             key_sum += jnp.dot(score_grad, two_heads(q_ref, part), preferred_element_type=jnp.float32)
             dq_acc[:, lanes] += jnp.dot(key_pair_t, score_grad, preferred_element_type=jnp.float32)
 
-        pair_acc[0, block_rows(2 * pair), :] = key_sum[:BLK]
-        pair_acc[1, block_rows(2 * pair), :] = value_sum[:BLK]
+        pair_acc[0, block_rows(2 * pair), :] = key_sum[:BLK].astype(pair_acc.dtype)
+        pair_acc[1, block_rows(2 * pair), :] = value_sum[:BLK].astype(pair_acc.dtype)
 
         @pl.when(2 * pair + 1 < count)
         def _():
-            pair_acc[0, block_rows(2 * pair + 1), :] = key_sum[BLK:]
-            pair_acc[1, block_rows(2 * pair + 1), :] = value_sum[BLK:]
+            pair_acc[0, block_rows(2 * pair + 1), :] = key_sum[BLK:].astype(pair_acc.dtype)
+            pair_acc[1, block_rows(2 * pair + 1), :] = value_sum[BLK:].astype(pair_acc.dtype)
 
         return carry
 
@@ -211,7 +211,7 @@
                 pltpu.VMEM((NBLK * BLK, LANES), jnp.float32),
                 pltpu.VMEM((NBLK, LANES), jnp.float32),
                 pltpu.VMEM((HEAD_DIM, LANES), jnp.float32),
-                pltpu.VMEM((2, NBLK * BLK, HEAD_DIM), jnp.float32),
+                pltpu.VMEM((2, NBLK * BLK, HEAD_DIM), jnp.bfloat16),
             ],
         ),
         out_shape=[

time: 120 us -> 120 us (level)
  starting transfers between devices: 58.3 us -> 55.8 us
  waiting for transfers between devices: 36.2 us -> 38.7 us
    ppermute x4, starting transfers between devices: 21.7 us -> 17.3 us  [to_previous_section(): lax.ppermute(block, 'section', [((s + 1) % sections, s) for s in range(se...]
    ppermute x18, waiting for transfers between devices: 31 us -> 33.5 us  [send(): return lax.ppermute(block, 'ctx', ctx_route(move))]
    ppermute x18, starting transfers between devices: 36.6 us -> 38.5 us  [send(): return lax.ppermute(block, 'ctx', ctx_route(move))]
where the time goes in v4:
time: 120 us; the launch traced here: 119 us
  starting transfers between devices  55.8 us (46%)
  waiting for transfers between devices  38.7 us (32%)
  Pallas kernels  16.3 us (14%)
  local copies, waits for them, and re-layouts  4.35 us (4%)
  other arithmetic  3.14 us (3%)
    ppermute x18, starting transfers between devices, send(): return lax.ppermute(block, 'ctx', ctx_route(move))  38.5 us
    ppermute x18, waiting for transfers between devices, send(): return lax.ppermute(block, 'ctx', ctx_route(move))  33.5 us
    ppermute x4, starting transfers between devices, to_previous_section(): lax.ppermute(block, 'section', [((s + 1) % sections, s) for s in range(se...  17.3 us
    pallas_call x3, Pallas kernels, chunk_grads(): pl.pallas_call(functools.partial(grads_kernel, by_block), grid_spec=pltpu...  16.3 us
    ppermute x4, waiting for transfers between devices, to_previous_section(): lax.ppermute(block, 'section', [((s + 1) % sections, s) for s in range(se...  5.24 us
  transfers between devices with their start and end apart: 22, of which 10 were waited for; matrix products, arithmetic and copies ran while one was open for 4% of the time, Pallas kernels for 14%

profile of v4, /device:TPU:2, one launch (start us, length us, event | category | flops | bytes accessed | tf_op | source)
XLA Modules:
  0.0 119.2 jit_solution(7107174103621223463)
XLA Ops:
  2.6 2.3 %collective-permute-start.1 = (bf16[2,128,1024]{2,1,0:T(8,128)(2,1)S(1)}, bf16[2,128,1024]{2,1,0:T(8,128)(2,1)S(1)}, u32[]{:S(2)}, u32[]{:S(2)}) collective-permute-start(bf16[2,128,1024]{2,1,0:T(8,128)(2,1)S(1)} %constant_dynamic-update-slice_fusion.own_ref), channel_id=1, source_target_pairs={{0,3},{1,0},{2,1},{3,2},{4,7},{5,4},{6,5},{7,6},{8,11},{9,8},{10,9... | collective-permute-start | bytes 1572872 | tf_op jit(solution)/shard_map/ppermute | solution.py:56
  4.9 3.3 %collective-permute-start.2 = (bf16[2,128,1024]{2,1,0:T(8,128)(2,1)S(1)}, bf16[2,128,1024]{2,1,0:T(8,128)(2,1)S(1)}, u32[]{:S(2)}, u32[]{:S(2)}) collective-permute-start(bf16[2,128,1024]{2,1,0:T(8,128)(2,1)S(1)} %constant_dynamic-update-slice_fusion.own_ref), channel_id=1, source_target_pairs={{0,4},{1,5},{2,6},{3,7},{8,12},{9,13},{10,14},{11,15},{16,20},{17,... | collective-permute-start | bytes 1572872 | tf_op jit(solution)/shard_map/ppermute | solution.py:56
  10.2 6.1 %collective-permute-done.1.right_ref = bf16[2,128,1024]{2,1,0:T(8,128)(2,1)S(1)} collective-permute-done((bf16[2,128,1024]{2,1,0:T(8,128)(2,1)S(1)}, bf16[2,128,1024]{2,1,0:T(8,128)(2,1)S(1)}, u32[]{:S(2)}, u32[]{:S(2)}) %collective-permute-start.1) | collective-permute-done | bytes 524320 | tf_op jit(solution)/shard_map/ppermute | solution.py:56
  17.7 3.5 %collective-permute-start.4 = (bf16[2,2,128,384]{3,2,1,0:T(8,128)(2,1)S(1)}, bf16[2,2,128,384]{3,2,1,0:T(8,128)(2,1)S(1)}, u32[]{:S(2)}, u32[]{:S(2)}) collective-permute-start(bf16[2,2,128,384]{3,2,1,0:T(8,128)(2,1)S(1)} %pad_maximum_fusion.3), channel_id=1, source_target_pairs={{0,4},{1,5},{2,6},{3,7},{8,12},{9,13},{10,14},{11,15},{16,20},{17,... | collective-permute-start | bytes 1179656 | tf_op jit(solution)/shard_map/ppermute | solution.py:56
  23.7 3.5 %collective-permute-start.7 = (bf16[2,2,128,640]{3,2,1,0:T(8,128)(2,1)S(1)}, bf16[2,2,128,640]{3,2,1,0:T(8,128)(2,1)S(1)}, u32[]{:S(2)}, u32[]{:S(2)}) collective-permute-start(bf16[2,2,128,640]{3,2,1,0:T(8,128)(2,1)S(1)} %pad_maximum_fusion.1), channel_id=1, source_target_pairs={{0,4},{1,5},{2,6},{3,7},{8,12},{9,13},{10,14},{11,15},{16,20},{17,... | collective-permute-start | bytes 1966088 | tf_op jit(solution)/shard_map/ppermute | solution.py:56
  27.6 3.2 %collective-permute-done.4.ylr_ref = bf16[2,2,128,384]{3,2,1,0:T(8,128)(2,1)S(1)} collective-permute-done((bf16[2,2,128,384]{3,2,1,0:T(8,128)(2,1)S(1)}, bf16[2,2,128,384]{3,2,1,0:T(8,128)(2,1)S(1)}, u32[]{:S(2)}, u32[]{:S(2)}) %collective-permute-start.4) | collective-permute-done | bytes 393248 | tf_op jit(solution)/shard_map/ppermute | solution.py:56
  30.7 4.2 %collective-permute-done.3.x2_ref = bf16[2,2,128,384]{3,2,1,0:T(8,128)(2,1)S(1)} collective-permute-done((bf16[2,2,128,384]{3,2,1,0:T(8,128)(2,1)S(1)}, bf16[2,2,128,384]{3,2,1,0:T(8,128)(2,1)S(1)}, u32[]{:S(2)}, u32[]{:S(2)}) %collective-permute-start.3) | collective-permute-done | bytes 393248 | tf_op jit(solution)/shard_map/ppermute | solution.py:56
  34.9 6.0 %shard_map.94 = (bf16[128,3072]{1,0:T(8,128)(2,1)S(1)}, bf16[2,2,128,384]{3,2,1,0:T(8,128)(2,1)S(1)}, bf16[2,2,128,384]{3,2,1,0:T(8,128)(2,1)S(1)}, bf16[2,2,128...) custom-call(s32[10]{0:T(128)S(1)} %pad_add_fusion.info, s32[8,128]{1,0:T(8,128)S(1)} %bitcast.35, ...), custom_call_target="tpu_custom_call" | custom-call | flops 20132659200 | bytes 2359296 | tf_op jit(solution)/shard_map/pallas_call | solution.py:198
  41.0 3.3 %collective-permute-start.5 = (bf16[128,3072]{1,0:T(8,128)(2,1)S(1)}, bf16[128,3072]{1,0:T(8,128)(2,1)S(1)}, u32[]{:S(2)}, u32[]{:S(2)}) collective-permute-start(bf16[128,3072]{1,0:T(8,128)(2,1)S(1)} %get-tuple-element.21), channel_id=1, source_target_pairs={{8,0},{16,8},{24,16},{32,24},{40,32},{48,40},{56,48},{64,56},{72,6... | collective-permute-start | bytes 2359304 | tf_op jit(solution)/shard_map/ppermute | solution.py:61
  44.2 4.2 %collective-permute-start.10 = (bf16[2,2,128,384]{3,2,1,0:T(8,128)(2,1)S(1)}, bf16[2,2,128,384]{3,2,1,0:T(8,128)(2,1)S(1)}, u32[]{:S(2)}, u32[]{:S(2)}) collective-permute-start(bf16[2,2,128,384]{3,2,1,0:T(8,128)(2,1)S(1)} %get-tuple-element.24), channel_id=1, source_target_pairs={{0,1},{1,2},{2,3},{3,0},{4,5},{5,6},{6,7},{7,4},{8,9},{9,10},{10,1... | collective-permute-start | bytes 1179656 | tf_op jit(solution)/shard_map/ppermute | solution.py:56
  49.7 2.6 %collective-permute-start.9 = (bf16[2,2,128,384]{3,2,1,0:T(8,128)(2,1)S(1)}, bf16[2,2,128,384]{3,2,1,0:T(8,128)(2,1)S(1)}, u32[]{:S(2)}, u32[]{:S(2)}) collective-permute-start(bf16[2,2,128,384]{3,2,1,0:T(8,128)(2,1)S(1)} %get-tuple-element.23), channel_id=1, source_target_pairs={{0,3},{1,0},{2,1},{3,2},{4,7},{5,4},{6,5},{7,6},{8,11},{9,8},{10,9... | collective-permute-start | bytes 1179656 | tf_op jit(solution)/shard_map/ppermute | solution.py:56
  52.4 6.0 %shard_map.95 = (bf16[128,3072]{1,0:T(8,128)(2,1)S(1)}, bf16[2,2,128,384]{3,2,1,0:T(8,128)(2,1)S(1)}, bf16[2,2,128,384]{3,2,1,0:T(8,128)(2,1)S(1)}, bf16[2,2,128...) custom-call(s32[10]{0:T(128)S(1)} %pad_add_fusion.info, s32[8,128]{1,0:T(8,128)S(1)} %bitcast.36, ...), custom_call_target="tpu_custom_call" | custom-call | flops 20132659200 | bytes 2359296 | tf_op jit(solution)/shard_map/pallas_call | solution.py:198
  59.3 3.3 %collective-permute-done.10 = bf16[2,2,128,384]{3,2,1,0:T(8,128)(2,1)S(1)} collective-permute-done((bf16[2,2,128,384]{3,2,1,0:T(8,128)(2,1)S(1)}, bf16[2,2,128,384]{3,2,1,0:T(8,128)(2,1)S(1)}, u32[]{:S(2)}, u32[]{:S(2)}) %collective-permute-start.10) | collective-permute-done | bytes 393248 | tf_op jit(solution)/shard_map/ppermute | solution.py:56
  62.5 3.0 %collective-permute-start.14 = (bf16[2,2,128,384]{3,2,1,0:T(8,128)(2,1)S(1)}, bf16[2,2,128,384]{3,2,1,0:T(8,128)(2,1)S(1)}, u32[]{:S(2)}, u32[]{:S(2)}) collective-permute-start(bf16[2,2,128,384]{3,2,1,0:T(8,128)(2,1)S(1)} %get-tuple-element.34), channel_id=1, source_target_pairs={{0,1},{1,2},{2,3},{3,0},{4,5},{5,6},{6,7},{7,4},{8,9},{9,10},{10,1... | collective-permute-start | bytes 1179656 | tf_op jit(solution)/shard_map/ppermute | solution.py:56
  67.7 4.8 %collective-permute-start.8 = (bf16[128,3072]{1,0:T(8,128)(2,1)S(1)}, bf16[128,3072]{1,0:T(8,128)(2,1)S(1)}, u32[]{:S(2)}, u32[]{:S(2)}) collective-permute-start(bf16[128,3072]{1,0:T(8,128)(2,1)S(1)} %get-tuple-element.22), channel_id=1, source_target_pairs={{8,0},{16,8},{24,16},{32,24},{40,32},{48,40},{56,48},{64,56},{72,6... | collective-permute-start | bytes 2359304 | tf_op jit(solution)/shard_map/ppermute | solution.py:61
  72.5 4.3 %shard_map.96 = (bf16[128,2048]{1,0:T(8,128)(2,1)S(1)}, bf16[2,2,128,256]{3,2,1,0:T(8,128)(2,1)S(1)}, bf16[2,2,128,256]{3,2,1,0:T(8,128)(2,1)S(1)}, bf16[2,2,128...) custom-call(s32[10]{0:T(128)S(1)} %pad_add_fusion.info, s32[8,128]{1,0:T(8,128)S(1)} %bitcast.37, ...), custom_call_target="tpu_custom_call" | custom-call | flops 13421772800 | bytes 1572864 | tf_op jit(solution)/shard_map/pallas_call | solution.py:198
  79.2 3.5 %collective-permute-start.17 = (bf16[2,2,128,256]{3,2,1,0:T(8,128)(2,1)S(1)}, bf16[2,2,128,256]{3,2,1,0:T(8,128)(2,1)S(1)}, u32[]{:S(2)}, u32[]{:S(2)}) collective-permute-start(bf16[2,2,128,256]{3,2,1,0:T(8,128)(2,1)S(1)} %get-tuple-element.37), channel_id=1, source_target_pairs={{0,1},{1,2},{2,3},{3,0},{4,5},{5,6},{6,7},{7,4},{8,9},{9,10},{10,1... | collective-permute-start | bytes 786440 | tf_op jit(solution)/shard_map/ppermute | solution.py:56
  82.8 3.3 %collective-permute-start.18 = (bf16[2,2,128,256]{3,2,1,0:T(8,128)(2,1)S(1)}, bf16[2,2,128,256]{3,2,1,0:T(8,128)(2,1)S(1)}, u32[]{:S(2)}, u32[]{:S(2)}) collective-permute-start(bf16[2,2,128,256]{3,2,1,0:T(8,128)(2,1)S(1)} %get-tuple-element.38), channel_id=1, source_target_pairs={{0,2},{1,3},{2,0},{3,1},{4,6},{5,7},{6,4},{7,5},{8,10},{9,11},{10,... | collective-permute-start | bytes 786440 | tf_op jit(solution)/shard_map/ppermute | solution.py:56
  87.6 3.5 %collective-permute-done.16 = bf16[2,2,128,256]{3,2,1,0:T(8,128)(2,1)S(1)} collective-permute-done((bf16[2,2,128,256]{3,2,1,0:T(8,128)(2,1)S(1)}, bf16[2,2,128,256]{3,2,1,0:T(8,128)(2,1)S(1)}, u32[]{:S(2)}, u32[]{:S(2)}) %collective-permute-start.16) | collective-permute-done | bytes 262176 | tf_op jit(solution)/shard_map/ppermute | solution.py:56
  91.1 4.1 %collective-permute-start.12 = (bf16[128,2048]{1,0:T(8,128)(2,1)S(1)}, bf16[128,2048]{1,0:T(8,128)(2,1)S(1)}, u32[]{:S(2)}, u32[]{:S(2)}) collective-permute-start(bf16[128,2048]{1,0:T(8,128)(2,1)S(1)} %get-tuple-element.27), channel_id=1, source_target_pairs={{8,0},{16,8},{24,16},{32,24},{40,32},{48,40},{56,48},{64,56},{72,6... | collective-permute-start | bytes 1572872 | tf_op jit(solution)/shard_map/ppermute | solution.py:61
  96.7 3.6 %collective-permute-done.19 = bf16[2,128,768]{2,1,0:T(8,128)(2,1)S(1)} collective-permute-done((bf16[2,128,768]{2,1,0:T(8,128)(2,1)S(1)}, bf16[2,128,768]{2,1,0:T(8,128)(2,1)S(1)}, u32[]{:S(2)}, u32[]{:S(2)}) %collective-permute-start.19) | collective-permute-done | bytes 393248 | tf_op jit(solution)/shard_map/ppermute | solution.py:56
  100.3 6.2 %collective-permute-done.20 = bf16[2,128,256]{2,1,0:T(8,128)(2,1)S(1)} collective-permute-done((bf16[2,128,256]{2,1,0:T(8,128)(2,1)S(1)}, bf16[2,128,256]{2,1,0:T(8,128)(2,1)S(1)}, u32[]{:S(2)}, u32[]{:S(2)}) %collective-permute-start.20) | collective-permute-done | bytes 131104 | tf_op jit(solution)/shard_map/ppermute | solution.py:56
  106.6 5.0 %collective-permute-start.21 = (bf16[2,128,1024]{2,1,0:T(8,128)(2,1)S(1)}, bf16[2,128,1024]{2,1,0:T(8,128)(2,1)S(1)}, u32[]{:S(2)}, u32[]{:S(2)}) collective-permute-start(bf16[2,128,1024]{2,1,0:T(8,128)(2,1)S(1)} %add_convert_fusion), channel_id=1, source_target_pairs={{8,0},{16,8},{24,16},{32,24},{40,32},{48,40},{56,48},{64,56},{72,6... | collective-permute-start | bytes 1572872 | tf_op jit(solution)/shard_map/ppermute | solution.py:61
  113.1 5.2 %collective-permute-done.21 = bf16[2,128,1024]{2,1,0:T(8,128)(2,1)S(1)} collective-permute-done((bf16[2,128,1024]{2,1,0:T(8,128)(2,1)S(1)}, bf16[2,128,1024]{2,1,0:T(8,128)(2,1)S(1)}, u32[]{:S(2)}, u32[]{:S(2)}) %collective-permute-start.21) | collective-permute-done | bytes 524320 | tf_op jit(solution)/shard_map/ppermute | solution.py:61
  (58 shorter events, 20.3 us)
Async XLA Ops:
  2.6 13.7 %collective-permute-start.1 = (bf16[2,128,1024]{2,1,0:T(8,128)(2,1)S(1)}, bf16[2,128,1024]{2,1,0:T(8,128)(2,1)S(1)}, u32[]{:S(2)}, u32[]{:S(2)}) collective-permute-start(bf16[2,128,1024]{2,1,0:T(8,128)(2,1)S(1)} %constant_dynamic-update-slice_fusion.own_ref), channel_id=1, source_target_pairs={{0,3},{1,0},{2,1},{3,2},{4,7},{5,4},{6,5},{7,6},{8,11},{9,8},{10,9... | collective-permute-start | bytes 1572872 | tf_op jit(solution)/shard_map/ppermute | solution.py:56
  4.9 12.7 %collective-permute-start = (bf16[2,128,1024]{2,1,0:T(8,128)(2,1)S(1)}, bf16[2,128,1024]{2,1,0:T(8,128)(2,1)S(1)}, u32[]{:S(2)}, u32[]{:S(2)}) collective-permute-start(bf16[2,128,1024]{2,1,0:T(8,128)(2,1)S(1)} %constant_dynamic-update-slice_fusion.own_ref), channel_id=1, source_target_pairs={{0,1},{1,2},{2,3},{3,0},{4,5},{5,6},{6,7},{7,4},{8,9},{9,10},{10,1... | collective-permute-start | bytes 1572872 | tf_op jit(solution)/shard_map/ppermute | solution.py:56
  4.9 16.3 %collective-permute-start.2 = (bf16[2,128,1024]{2,1,0:T(8,128)(2,1)S(1)}, bf16[2,128,1024]{2,1,0:T(8,128)(2,1)S(1)}, u32[]{:S(2)}, u32[]{:S(2)}) collective-permute-start(bf16[2,128,1024]{2,1,0:T(8,128)(2,1)S(1)} %constant_dynamic-update-slice_fusion.own_ref), channel_id=1, source_target_pairs={{0,4},{1,5},{2,6},{3,7},{8,12},{9,13},{10,14},{11,15},{16,20},{17,... | collective-permute-start | bytes 1572872 | tf_op jit(solution)/shard_map/ppermute | solution.py:56
  17.7 13.0 %collective-permute-start.4 = (bf16[2,2,128,384]{3,2,1,0:T(8,128)(2,1)S(1)}, bf16[2,2,128,384]{3,2,1,0:T(8,128)(2,1)S(1)}, u32[]{:S(2)}, u32[]{:S(2)}) collective-permute-start(bf16[2,2,128,384]{3,2,1,0:T(8,128)(2,1)S(1)} %pad_maximum_fusion.3), channel_id=1, source_target_pairs={{0,4},{1,5},{2,6},{3,7},{8,12},{9,13},{10,14},{11,15},{16,20},{17,... | collective-permute-start | bytes 1179656 | tf_op jit(solution)/shard_map/ppermute | solution.py:56
  21.3 13.6 %collective-permute-start.3 = (bf16[2,2,128,384]{3,2,1,0:T(8,128)(2,1)S(1)}, bf16[2,2,128,384]{3,2,1,0:T(8,128)(2,1)S(1)}, u32[]{:S(2)}, u32[]{:S(2)}) collective-permute-start(bf16[2,2,128,384]{3,2,1,0:T(8,128)(2,1)S(1)} %pad_maximum_fusion.2), channel_id=1, source_target_pairs={{0,2},{1,3},{2,0},{3,1},{4,6},{5,7},{6,4},{7,5},{8,10},{9,11},{10,... | collective-permute-start | bytes 1179656 | tf_op jit(solution)/shard_map/ppermute | solution.py:56
  23.5 11.5 %copy-start.2 = (bf16[1,128,8192]{2,1,0:T(8,128)(2,1)S(1)}, bf16[1,128,8192]{2,1,0:T(8,128)(2,1)}, u32[]{:S(2)}) copy-start(bf16[1,128,8192]{2,1,0:T(8,128)(2,1)} %g_ref.5) | copy-start | bytes 6291460
  23.5 11.4 %copy-start.1 = (bf16[1,128,8192]{2,1,0:T(8,128)(2,1)S(1)}, bf16[1,128,8192]{2,1,0:T(8,128)(2,1)}, u32[]{:S(2)}) copy-start(bf16[1,128,8192]{2,1,0:T(8,128)(2,1)} %q_ref.5) | copy-start | bytes 6291460
  23.7 26.1 %collective-permute-start.7 = (bf16[2,2,128,640]{3,2,1,0:T(8,128)(2,1)S(1)}, bf16[2,2,128,640]{3,2,1,0:T(8,128)(2,1)S(1)}, u32[]{:S(2)}, u32[]{:S(2)}) collective-permute-start(bf16[2,2,128,640]{3,2,1,0:T(8,128)(2,1)S(1)} %pad_maximum_fusion.1), channel_id=1, source_target_pairs={{0,4},{1,5},{2,6},{3,7},{8,12},{9,13},{10,14},{11,15},{16,20},{17,... | collective-permute-start | bytes 1966088 | tf_op jit(solution)/shard_map/ppermute | solution.py:56
  27.3 25.1 %collective-permute-start.6 = (bf16[2,2,128,640]{3,2,1,0:T(8,128)(2,1)S(1)}, bf16[2,2,128,640]{3,2,1,0:T(8,128)(2,1)S(1)}, u32[]{:S(2)}, u32[]{:S(2)}) collective-permute-start(bf16[2,2,128,640]{3,2,1,0:T(8,128)(2,1)S(1)} %pad_maximum_fusion), channel_id=1, source_target_pairs={{0,2},{1,3},{2,0},{3,1},{4,6},{5,7},{6,4},{7,5},{8,10},{9,11},{10,... | collective-permute-start | bytes 1966088 | tf_op jit(solution)/shard_map/ppermute | solution.py:56
  41.0 31.6 %collective-permute-start.5 = (bf16[128,3072]{1,0:T(8,128)(2,1)S(1)}, bf16[128,3072]{1,0:T(8,128)(2,1)S(1)}, u32[]{:S(2)}, u32[]{:S(2)}) collective-permute-start(bf16[128,3072]{1,0:T(8,128)(2,1)S(1)} %get-tuple-element.21), channel_id=1, source_target_pairs={{8,0},{16,8},{24,16},{32,24},{40,32},{48,40},{56,48},{64,56},{72,6... | collective-permute-start | bytes 2359304 | tf_op jit(solution)/shard_map/ppermute | solution.py:61
  44.2 18.3 %collective-permute-start.10 = (bf16[2,2,128,384]{3,2,1,0:T(8,128)(2,1)S(1)}, bf16[2,2,128,384]{3,2,1,0:T(8,128)(2,1)S(1)}, u32[]{:S(2)}, u32[]{:S(2)}) collective-permute-start(bf16[2,2,128,384]{3,2,1,0:T(8,128)(2,1)S(1)} %get-tuple-element.24), channel_id=1, source_target_pairs={{0,1},{1,2},{2,3},{3,0},{4,5},{5,6},{6,7},{7,4},{8,9},{9,10},{10,1... | collective-permute-start | bytes 1179656 | tf_op jit(solution)/shard_map/ppermute | solution.py:56
  48.4 17.1 %collective-permute-start.11 = (bf16[2,2,128,384]{3,2,1,0:T(8,128)(2,1)S(1)}, bf16[2,2,128,384]{3,2,1,0:T(8,128)(2,1)S(1)}, u32[]{:S(2)}, u32[]{:S(2)}) collective-permute-start(bf16[2,2,128,384]{3,2,1,0:T(8,128)(2,1)S(1)} %get-tuple-element.25), channel_id=1, source_target_pairs={{0,2},{1,3},{2,0},{3,1},{4,6},{5,7},{6,4},{7,5},{8,10},{9,11},{10,... | collective-permute-start | bytes 1179656 | tf_op jit(solution)/shard_map/ppermute | solution.py:56
  49.7 18.0 %collective-permute-start.9 = (bf16[2,2,128,384]{3,2,1,0:T(8,128)(2,1)S(1)}, bf16[2,2,128,384]{3,2,1,0:T(8,128)(2,1)S(1)}, u32[]{:S(2)}, u32[]{:S(2)}) collective-permute-start(bf16[2,2,128,384]{3,2,1,0:T(8,128)(2,1)S(1)} %get-tuple-element.23), channel_id=1, source_target_pairs={{0,3},{1,0},{2,1},{3,2},{4,7},{5,4},{6,5},{7,6},{8,11},{9,8},{10,9... | collective-permute-start | bytes 1179656 | tf_op jit(solution)/shard_map/ppermute | solution.py:56
  58.4 20.8 %collective-permute-start.13 = (bf16[2,2,128,384]{3,2,1,0:T(8,128)(2,1)S(1)}, bf16[2,2,128,384]{3,2,1,0:T(8,128)(2,1)S(1)}, u32[]{:S(2)}, u32[]{:S(2)}) collective-permute-start(bf16[2,2,128,384]{3,2,1,0:T(8,128)(2,1)S(1)} %get-tuple-element.33), channel_id=1, source_target_pairs={{0,3},{1,0},{2,1},{3,2},{4,7},{5,4},{6,5},{7,6},{8,11},{9,8},{10,9... | collective-permute-start | bytes 1179656 | tf_op jit(solution)/shard_map/ppermute | solution.py:56
  62.5 20.2 %collective-permute-start.14 = (bf16[2,2,128,384]{3,2,1,0:T(8,128)(2,1)S(1)}, bf16[2,2,128,384]{3,2,1,0:T(8,128)(2,1)S(1)}, u32[]{:S(2)}, u32[]{:S(2)}) collective-permute-start(bf16[2,2,128,384]{3,2,1,0:T(8,128)(2,1)S(1)} %get-tuple-element.34), channel_id=1, source_target_pairs={{0,1},{1,2},{2,3},{3,0},{4,5},{5,6},{6,7},{7,4},{8,9},{9,10},{10,1... | collective-permute-start | bytes 1179656 | tf_op jit(solution)/shard_map/ppermute | solution.py:56
  65.5 20.5 %collective-permute-start.15 = (bf16[2,2,128,384]{3,2,1,0:T(8,128)(2,1)S(1)}, bf16[2,2,128,384]{3,2,1,0:T(8,128)(2,1)S(1)}, u32[]{:S(2)}, u32[]{:S(2)}) collective-permute-start(bf16[2,2,128,384]{3,2,1,0:T(8,128)(2,1)S(1)} %get-tuple-element.35), channel_id=1, source_target_pairs={{0,2},{1,3},{2,0},{3,1},{4,6},{5,7},{6,4},{7,5},{8,10},{9,11},{10,... | collective-permute-start | bytes 1179656 | tf_op jit(solution)/shard_map/ppermute | solution.py:56
  67.7 43.9 %collective-permute-start.8 = (bf16[128,3072]{1,0:T(8,128)(2,1)S(1)}, bf16[128,3072]{1,0:T(8,128)(2,1)S(1)}, u32[]{:S(2)}, u32[]{:S(2)}) collective-permute-start(bf16[128,3072]{1,0:T(8,128)(2,1)S(1)} %get-tuple-element.22), channel_id=1, source_target_pairs={{8,0},{16,8},{24,16},{32,24},{40,32},{48,40},{56,48},{64,56},{72,6... | collective-permute-start | bytes 2359304 | tf_op jit(solution)/shard_map/ppermute | solution.py:61
  76.8 14.2 %collective-permute-start.16 = (bf16[2,2,128,256]{3,2,1,0:T(8,128)(2,1)S(1)}, bf16[2,2,128,256]{3,2,1,0:T(8,128)(2,1)S(1)}, u32[]{:S(2)}, u32[]{:S(2)}) collective-permute-start(bf16[2,2,128,256]{3,2,1,0:T(8,128)(2,1)S(1)} %get-tuple-element.36), channel_id=1, source_target_pairs={{0,3},{1,0},{2,1},{3,2},{4,7},{5,4},{6,5},{7,6},{8,11},{9,8},{10,9... | collective-permute-start | bytes 786440 | tf_op jit(solution)/shard_map/ppermute | solution.py:56
  79.2 16.0 %collective-permute-start.17 = (bf16[2,2,128,256]{3,2,1,0:T(8,128)(2,1)S(1)}, bf16[2,2,128,256]{3,2,1,0:T(8,128)(2,1)S(1)}, u32[]{:S(2)}, u32[]{:S(2)}) collective-permute-start(bf16[2,2,128,256]{3,2,1,0:T(8,128)(2,1)S(1)} %get-tuple-element.37), channel_id=1, source_target_pairs={{0,1},{1,2},{2,3},{3,0},{4,5},{5,6},{6,7},{7,4},{8,9},{9,10},{10,1... | collective-permute-start | bytes 786440 | tf_op jit(solution)/shard_map/ppermute | solution.py:56
  82.8 12.4 %collective-permute-start.18 = (bf16[2,2,128,256]{3,2,1,0:T(8,128)(2,1)S(1)}, bf16[2,2,128,256]{3,2,1,0:T(8,128)(2,1)S(1)}, u32[]{:S(2)}, u32[]{:S(2)}) collective-permute-start(bf16[2,2,128,256]{3,2,1,0:T(8,128)(2,1)S(1)} %get-tuple-element.38), channel_id=1, source_target_pairs={{0,2},{1,3},{2,0},{3,1},{4,6},{5,7},{6,4},{7,5},{8,10},{9,11},{10,... | collective-permute-start | bytes 786440 | tf_op jit(solution)/shard_map/ppermute | solution.py:56
  86.3 14.0 %collective-permute-start.19 = (bf16[2,128,768]{2,1,0:T(8,128)(2,1)S(1)}, bf16[2,128,768]{2,1,0:T(8,128)(2,1)S(1)}, u32[]{:S(2)}, u32[]{:S(2)}) collective-permute-start(bf16[2,128,768]{2,1,0:T(8,128)(2,1)S(1)} %pad_maximum_fusion.4), channel_id=1, source_target_pairs={{4,0},{5,1},{6,2},{7,3},{12,8},{13,9},{14,10},{15,11},{20,16},{21,... | collective-permute-start | bytes 1179656 | tf_op jit(solution)/shard_map/ppermute | solution.py:56
  91.1 20.6 %collective-permute-start.12 = (bf16[128,2048]{1,0:T(8,128)(2,1)S(1)}, bf16[128,2048]{1,0:T(8,128)(2,1)S(1)}, u32[]{:S(2)}, u32[]{:S(2)}) collective-permute-start(bf16[128,2048]{1,0:T(8,128)(2,1)S(1)} %get-tuple-element.27), channel_id=1, source_target_pairs={{8,0},{16,8},{24,16},{32,24},{40,32},{48,40},{56,48},{64,56},{72,6... | collective-permute-start | bytes 1572872 | tf_op jit(solution)/shard_map/ppermute | solution.py:61
  95.4 11.1 %collective-permute-start.20 = (bf16[2,128,256]{2,1,0:T(8,128)(2,1)S(1)}, bf16[2,128,256]{2,1,0:T(8,128)(2,1)S(1)}, u32[]{:S(2)}, u32[]{:S(2)}) collective-permute-start(bf16[2,128,256]{2,1,0:T(8,128)(2,1)S(1)} %get-tuple-element.45), channel_id=1, source_target_pairs={{4,0},{5,1},{6,2},{7,3},{12,8},{13,9},{14,10},{15,11},{20,16},{21,... | collective-permute-start | bytes 393224 | tf_op jit(solution)/shard_map/ppermute | solution.py:56
  106.6 11.7 %collective-permute-start.21 = (bf16[2,128,1024]{2,1,0:T(8,128)(2,1)S(1)}, bf16[2,128,1024]{2,1,0:T(8,128)(2,1)S(1)}, u32[]{:S(2)}, u32[]{:S(2)}) collective-permute-start(bf16[2,128,1024]{2,1,0:T(8,128)(2,1)S(1)} %add_convert_fusion), channel_id=1, source_target_pairs={{8,0},{16,8},{24,16},{32,24},{40,32},{48,40},{56,48},{64,56},{72,6... | collective-permute-start | bytes 1572872 | tf_op jit(solution)/shard_map/ppermute | solution.py:61
  (2 other events, 20.3 us)
